TPU v7x, 128 devices: a whole 4x4x4 slice. The times are simulated.
128 devices in a mesh: section: 2 (over x_hi), dp: 8 (over z, core), fsdp: 8 (over x_lo, y).
Axes of the slice: x: 4 (x_hi: 2, x_lo: 2; x = x_hi * 2 + x_lo), y: 4, z: 4, core: 2. Of those that a mesh axis runs over, the one named last changes fastest.
Arguments:
- inputs: bfloat16 [2, 8, 1024, 960], P(None, 'dp', 'fsdp'), may hold values from -6 to 6
- positions: int32 [2, 8, 1024], P(None, 'dp', 'fsdp'), may hold values from 0 to 2046, as said below
- plan: int32 [8, 2], P('dp'), may hold values from 0 to 1, as said below
- attend_in: bfloat16 [2, 960, 1600], P('section', 'fsdp'), may hold values from -0.1875 to 0.1875
- attend_out: bfloat16 [2, 960, 960], P('section', 'fsdp'), may hold values from -1 to 1
- gate_up: bfloat16 [2, 960, 5120], P('section', 'fsdp'), may hold values from -0.1875 to 0.1875
- down_weight: bfloat16 [2, 2560, 960], P('section', 'fsdp'), may hold values from -0.25 to 0.25
- norm_gains: bfloat16 [2, 2, 960], P('section', None, 'fsdp'), may hold values from 0.25 to 1.75
- cotangent: bfloat16 [2, 8, 1024, 960], P(None, 'dp', 'fsdp'), may hold values from -6 to 6
Outputs:
- activations: bfloat16 [2, 2, 8, 1024, 960], P('section', None, 'dp', 'fsdp')
- input_grads: float32 [2, 2, 8, 1024, 960], P('section', None, 'dp', 'fsdp')
- attend_in_gradient: float32 [2, 960, 1600], P('section', 'fsdp')
- attend_out_gradient: float32 [2, 960, 960], P('section', 'fsdp')
- gate_up_gradient: float32 [2, 960, 5120], P('section', 'fsdp')
- down_gradient: float32 [2, 2560, 960], P('section', 'fsdp')
- gains_gradient: float32 [2, 2, 960], P('section', None, 'fsdp')
Inputs may be any that keep to these rules, and one draw needn't show every extreme that they name: Along each sequence the positions start at 0, rise by 1 to 3 from token to token, and end at 2046. `plan`: each row is a permutation of 0 .. 1.
All inputs are finite; a program needn't handle non-finite values.
Results may differ from a plain program's by a relative error of at most 0.025.
Values may be sent and summed in bfloat16 or wider, within the bound.
A program may use at most 256 MiB of HBM per device.

v0:
```python
import functools

import jax
import jax.numpy as jnp
from jax import lax
from jax.experimental import pallas as pl
from jax.experimental.pallas import tpu as pltpu
from jax.sharding import PartitionSpec as P

D = 960
QUERY_HEADS = 15
KEY_VALUE_HEADS = 5
HEAD_WIDTH = 64
FF = 2560
QUERY_WIDTH = QUERY_HEADS * HEAD_WIDTH
KEY_WIDTH = KEY_VALUE_HEADS * HEAD_WIDTH
QKV = QUERY_WIDTH + 2 * KEY_WIDTH
SHARDS = 8
ROWS = D // SHARDS
PADDED = 128
MODEL = 1024
PAIR = 2 * HEAD_WIDTH
FULL = SHARDS * PAIR
WIDE = FULL + KEY_VALUE_HEADS * PAIR

EPSILON = 1e-05
BASE = 10000.0

MESH = pl.DeviceIdType.MESH
ANY = pl.BlockSpec(memory_space=pl.ANY)
VMEM = pl.BlockSpec(memory_space=pltpu.VMEM)

GATE_UP = (PADDED, 2 * FF, "columns", FF, 0)
GATE_UP_FIRST = (PADDED, FF, "columns", FF, 0)
GATE_UP_SECOND = (PADDED, FF, "columns", FF, FF // 2)
DOWN = (FF // SHARDS, SHARDS * PADDED, "columns", SHARDS * PADDED // 2, 0)
ATTEND_IN = (PADDED, WIDE, "rows", 0, 0)
ATTEND_OUT = (PADDED, SHARDS * PADDED, "rows", 0, 0)
FEED_FORWARD = (GATE_UP, DOWN)
FEED_FORWARD_BACK = (GATE_UP_FIRST, GATE_UP_SECOND, DOWN)
ATTENTION = (ATTEND_IN, ATTEND_OUT)


def half_lanes(shape, core):
    _, columns, _, stride, offset = shape
    return pl.ds(pl.multiple_of(core * stride + offset, 128), columns // 2)


def half_shape(shape):
    rows, columns, kind = shape[:3]
    return (rows // 2, columns) if kind == "rows" else (rows, columns // 2)


def half_view(shape, core, start, count):
    rows, columns, kind = shape[:3]
    if kind == "rows":
        first = pl.multiple_of(core * (rows // 2) + start, 16)
        return (pl.ds(first, count), slice(None))
    return (pl.ds(pl.multiple_of(start, 16), count), half_lanes(shape, core))


def places():
    dp = lax.axis_index("dp")
    fsdp = lax.axis_index("fsdp")
    return dp // 2, dp % 2, fsdp // 4, fsdp % 4


def peer_ids():
    z, core, x, y = places()
    return {
        "X": {"fsdp": (1 - x) * 4 + y},
        "Yp": {"fsdp": x * 4 + (y + 1) % 4},
        "Ym": {"fsdp": x * 4 + (y + 3) % 4},
        "C": {"dp": z * 2 + 1 - core},
        "Z1": {"dp": ((z + 1) % 4) * 2 + core},
        "Z2": {"dp": ((z + 2) % 4) * 2 + core},
        "Z3": {"dp": ((z + 3) % 4) * 2 + core},
    }


def greet(ids, names):
    barrier = pltpu.get_barrier_semaphore()
    for name in names:
        pl.semaphore_signal(barrier, inc=1, device_id=ids[name], device_id_type=MESH)
    pl.semaphore_wait(barrier, len(names))


GATHER = (
    ("X", 0, 0, "f"),
    ("Yp", 0, 0, "f"),
    ("Ym", 0, 0, "f"),
    ("Ym", 0, 1, 0),
    ("X", 0, 1, 0),
    ("Yp", 0, 3, 1),
    ("X", 0, 3, 0),
    ("Yp", 1, 0, 1),
    ("Ym", 1, 0, 1),
    ("Ym", 1, 1, 0),
    ("Yp", 1, 3, 1),
)
GATHER_NEXT = {1: (5, 6), 2: (3, 4), 0: (7, 8), 4: (9,), 7: (10,)}
GATHER_STAGES = ((1, 2, 0), (4, 7, 3, 5, 6, 8), (9, 10))
GATHER_ORDER = (1, 2, 0, 4, 7, 3, 5, 6, 8, 9, 10)


def seen_by_receiver(peer, column, step):
    if peer == "X":
        return 1 - column, step
    if peer == "Yp":
        return column, (step + 3) % 4
    if peer == "Ym":
        return column, (step + 1) % 4
    return column, step


def part_rows(shape, part):
    rows = half_shape(shape)[0]
    return (0, rows) if part == "f" else (part * (rows // 2), rows // 2)


UPWARD = (0, 1, 3, 5, 7)
PLAIN_EDGES = 22
SPREAD_EDGES = 88


class Gather:
    def __init__(self, shapes, spread, shards, outs, sems):
        self.shapes, self.spread, self.shards, self.outs = shapes, spread, shards, outs
        self.local_sem, self.send_sem, self.recv_sem = sems
        self.z, self.core, self.x, self.y = places()
        self.ids = peer_ids()

    def owner(self, column, step):
        return ((self.x + column) % 2) * 4 + (self.y + step) % 4

    def index(self, array, part, which, plane):
        shape = self.shapes[array]
        start, rows = part_rows(shape, part)
        if array == self.spread:
            quarter = half_shape(shape)[0] // 4
            start, rows = plane * quarter + start // 4, rows // 4
        return half_view(shape, which, start, rows)

    def view(self, array, column, step, part, which, plane):
        return self.outs[array].at[
            (self.owner(column, step),) + self.index(array, part, which, plane)
        ]

    def received(self, edge):
        group, base = edge // 11, edge % 11
        peer, column, step, part = GATHER[base]
        column, step = seen_by_receiver(peer, column, step)
        return column, step, part, (0, 0, 3, 1, 2, 3, 1, 2)[group]

    def peer_of(self, edge):
        group, base = edge // 11, edge % 11
        if group == 0:
            return GATHER[base][0]
        if group in (1, 5, 6, 7):
            return "C"
        return {2: "Z1", 3: "Z3", 4: "Z1" if base in UPWARD else "Z3"}[group]

    def copy(self, array, edge):
        group, base = edge // 11, edge % 11
        if group == 0:
            _, column, step, part = GATHER[base]
            away = 0
        else:
            column, step, part, away = self.received(edge)
            if group in (2, 3):
                away = 0
            elif group == 4:
                away = 3 if base in UPWARD else 1
        target = source = self.view(array, column, step, part, self.core, (self.z + away) % 4)
        if group == 0 and (column, step) == (0, 0):
            source = self.shards[array].at[self.index(array, part, self.core, self.z)]
        return pltpu.make_async_remote_copy(
            src_ref=source,
            dst_ref=target,
            send_sem=self.send_sem.at[array, edge],
            recv_sem=self.recv_sem.at[array, edge],
            device_id=self.ids[self.peer_of(edge)],
            device_id_type=MESH,
        )

    def wait_for(self, array, edge):
        column, step, part, away = self.received(edge)
        which = 1 - self.core if edge // 11 in (1, 5, 6, 7) else self.core
        landed = self.view(array, column, step, part, which, (self.z + away) % 4)
        pltpu.make_async_remote_copy(
            src_ref=landed,
            dst_ref=landed,
            send_sem=self.send_sem.at[array, edge],
            recv_sem=self.recv_sem.at[array, edge],
            device_id=self.ids["C"],
            device_id_type=MESH,
        ).wait_recv()

    def own(self, array):
        return pltpu.make_async_copy(
            self.shards[array],
            self.outs[array].at[self.x * 4 + self.y],
            self.local_sem.at[array],
        )

    def start(self):
        for array in range(len(self.shapes)):
            for edge in (0, 1, 2):
                self.copy(array, edge).start()
            self.own(array).start()

    def within_plane(self, array, edges):
        for edge in edges:
            self.wait_for(array, edge)
            for later in GATHER_NEXT.get(edge, ()):
                self.copy(array, later).start()
            if array == self.spread:
                self.copy(array, 22 + edge).start()
                self.copy(array, 33 + edge).start()
            self.copy(array, 11 + edge).start()

    def round_z(self, edges):
        if self.spread is None:
            return
        for edge in edges:
            for group in (2, 3):
                self.wait_for(self.spread, 11 * group + edge)
                if (group == 2) == (edge in UPWARD):
                    self.copy(self.spread, 44 + edge).start()
                self.copy(self.spread, 11 * (group + 3) + edge).start()

    def steps(self):
        first, second, third = GATHER_STAGES
        arrays = range(len(self.shapes))
        steps = [functools.partial(self.within_plane, array, first) for array in arrays]
        steps.append(functools.partial(self.round_z, first))
        steps += [functools.partial(self.within_plane, array, second) for array in arrays]
        steps.append(functools.partial(self.round_z, second))
        steps += [functools.partial(self.within_plane, array, third) for array in arrays]
        steps.append(functools.partial(self.round_z, third))
        steps.append(self.finish)
        return steps

    def finish(self):
        if self.spread is not None:
            for edge in GATHER_ORDER:
                self.wait_for(self.spread, 44 + edge)
                self.copy(self.spread, 77 + edge).start()
        for array in range(len(self.shapes)):
            last = SPREAD_EDGES if array == self.spread else PLAIN_EDGES
            for edge in range(last):
                if edge // 11 in (1, 5, 6, 7):
                    self.wait_for(array, edge)
            for edge in range(last):
                self.copy(array, edge).wait_send()
            self.own(array).wait()

    @staticmethod
    def out_shapes(shapes):
        return [
            jax.ShapeDtypeStruct((SHARDS, rows, columns), jnp.bfloat16)
            for rows, columns, *_ in shapes
        ]

    @staticmethod
    def scratch(shapes, spread):
        edges = PLAIN_EDGES if spread is None else SPREAD_EDGES
        return [
            pltpu.SemaphoreType.DMA((len(shapes),)),
            pltpu.SemaphoreType.DMA((len(shapes), edges)),
            pltpu.SemaphoreType.DMA((len(shapes), edges)),
        ]


def gather_kernel(shapes, *refs):
    count = len(shapes)
    gather = Gather(shapes, None, refs[:count], refs[count : 2 * count], refs[2 * count :])
    greet(gather.ids, ("X", "Yp", "Ym", "C"))
    gather.start()
    for step in gather.steps():
        step()


def gather_weights(shards):
    count = len(ATTENTION)
    return pl.pallas_call(
        functools.partial(gather_kernel, ATTENTION),
        name="gather_weights",
        out_shape=Gather.out_shapes(ATTENTION),
        in_specs=[VMEM] * count,
        out_specs=[ANY] * count,
        scratch_shapes=Gather.scratch(ATTENTION, None),
        compiler_params=pltpu.CompilerParams(collective_id=0, has_side_effects=True),
    )(*shards)


REDUCE = (
    ("Yp", 0, 2, 0, ()),
    ("Ym", 0, 2, 1, ()),
    ("Yp", 1, 2, 0, ()),
    ("Ym", 1, 2, 1, ()),
    ("X", 1, 3, 0, ()),
    ("Yp", 1, 1, 1, ()),
    ("X", 1, 1, 0, (2,)),
    ("Ym", 1, 3, 1, (3,)),
    ("Yp", 0, 1, "f", (0, 6)),
    ("Ym", 0, 3, "f", (1, 4)),
    ("X", 1, 0, "f", (5, 7)),
)
REDUCE_STAGES = ((0, 1, 2, 3, 4, 5), (6, 7), (8, 9, 10))
SHARD_ORDER = ((0, 2), (1, 2), (1, 3), (1, 1), (0, 1), (0, 3), (1, 0), (0, 0))
REDUCE_EDGES = 47
SLOTS = 2
ROWS_HERE = 256


class Reduce:
    def __init__(self, shapes, spread, lefts, rights, extra, outs, scratch):
        count = len(shapes)
        if len(lefts) < count:
            lefts, rights, outs = ((refs[0],) + tuple(refs) for refs in (lefts, rights, outs))
        self.shapes, self.spread, self.outs = shapes, spread, outs
        self.lefts, self.rights, self.extra = lefts, rights, extra
        self.totals = scratch[:count]
        self.wholes = scratch[count : 2 * count]
        self.parts = scratch[2 * count : 3 * count]
        self.quarters = scratch[3 * count : 4 * count]
        self.rounds = None if spread is None else scratch[4 * count]
        self.left_all = list(scratch[-4 - 2 * count : -4 - count])
        self.sides = [(0, 1)] * count
        if shapes[0] is GATE_UP_FIRST:
            self.left_all[1] = self.left_all[0]
            self.sides[1] = (1,)
        self.right_all = scratch[-4 - count : -4]
        self.operand_sem, self.local_sem, self.send_sem, self.recv_sem = scratch[-4:]
        self.z, self.core, self.x, self.y = places()
        self.mine = self.x * 4 + self.y
        self.ids = peer_ids()
        self.plain = [array for array in range(count) if array != spread]

    @staticmethod
    def piece_shapes(shapes, spread):
        halves = [half_shape(shape) for shape in shapes]
        return halves, [
            (half[0], half[1] // 4) if array == spread else half
            for array, half in enumerate(halves)
        ]

    @staticmethod
    def left_shape(shape, half):
        if shape is GATE_UP_SECOND:
            return (16, 128)
        if half[0] == PADDED:
            return (ROWS_HERE, SHARDS * PADDED)
        return (SHARDS, ROWS_HERE, half[0])

    @staticmethod
    def out_shapes(shapes):
        return [jax.ShapeDtypeStruct((rows, columns), jnp.bfloat16) for rows, columns, *_ in shapes]

    @staticmethod
    def scratch(shapes, spread):
        halves, pieces = Reduce.piece_shapes(shapes, spread)
        bf16 = jnp.bfloat16
        buffers = [pltpu.VMEM((SHARDS,) + half, bf16) for half in halves]
        buffers += [pltpu.VMEM((3,) + piece, bf16) for piece in pieces]
        buffers += [pltpu.VMEM((8, piece[0] // 2, piece[1]), bf16) for piece in pieces]
        buffers += [pltpu.VMEM((3, half[0] // 4, half[1]), bf16) for half in halves]
        if spread is not None:
            buffers.append(pltpu.VMEM((3 * SHARDS,) + pieces[spread], bf16))
        buffers += [
            pltpu.VMEM((2,) + Reduce.left_shape(shape, half), bf16)
            for shape, half in zip(shapes, halves)
        ]
        buffers += [pltpu.VMEM((2, ROWS_HERE, half[1]), bf16) for half in halves]
        return buffers + [
            pltpu.SemaphoreType.DMA((len(shapes), 2)),
            pltpu.SemaphoreType.DMA((len(shapes),)),
            pltpu.SemaphoreType.DMA((len(shapes), REDUCE_EDGES)),
            pltpu.SemaphoreType.DMA((len(shapes), REDUCE_EDGES)),
        ]

    def owner(self, column, step):
        return ((self.x + column) % 2) * 4 + (self.y + step) % 4

    def lanes(self, array, plane):
        columns = half_shape(self.shapes[array])[1]
        if array != self.spread:
            return pl.ds(0, columns)
        return pl.ds(pl.multiple_of(plane * (columns // 4), 128), columns // 4)

    def piece(self, array, edge):
        _, column, step, part, _ = REDUCE[edge]
        start, rows = part_rows(self.shapes[array], part)
        return self.totals[array].at[
            self.owner(column, step), pl.ds(start, rows), self.lanes(array, self.z)
        ]

    def slot(self, array, edge):
        return self.parts[array].at[edge] if edge < 8 else self.wholes[array].at[edge - 8]

    def add(self, array, into, start, rows, lanes, source):
        total = self.totals[array]

        @pl.loop(0, rows // 16)
        def _(index):
            offset = pl.multiple_of(index * 16, 16)
            at = pl.ds(pl.multiple_of(start + offset, 16), 16)
            total[into, at, lanes] = (
                total[into, at, lanes].astype(jnp.float32)
                + source[pl.ds(offset, 16), :].astype(jnp.float32)
            ).astype(jnp.bfloat16)

    def quarter(self, array, plane):
        rows = half_shape(self.shapes[array])[0]
        if array == self.spread:
            return 0, rows, self.lanes(array, plane)
        return pl.multiple_of(plane * (rows // 4), 16), rows // 4, self.lanes(array, plane)

    def summed(self, array, plane):
        start, rows, lanes = self.quarter(array, plane)
        return self.totals[array].at[self.mine, pl.ds(start, rows), lanes]

    def out_view(self, array, plane, which):
        shape = self.shapes[array]
        if array == self.spread:
            rows, columns = half_shape(shape)
            first = pl.multiple_of(which * shape[3] + shape[4] + plane * (columns // 4), 128)
            return self.outs[array].at[pl.ds(0, rows), pl.ds(first, columns // 4)]
        start, rows, _ = self.quarter(array, plane)
        return self.outs[array].at[half_view(shape, which, start, rows)]

    def copy(self, array, edge):
        z = self.z
        if edge < 11:
            peer, source, target = REDUCE[edge][0], self.piece(array, edge), self.slot(array, edge)
        elif edge < 14:
            step = edge - 10
            peer, source = f"Z{step}", self.summed(array, (z + step) % 4)
            target = self.quarters[array].at[step - 1]
        elif edge < 17:
            peer, source = f"Z{edge - 13}", self.summed(array, z)
            target = self.out_view(array, z, self.core)
        elif edge < 21:
            peer = "C"
            source = target = self.out_view(array, (z + edge - 17) % 4, self.core)
            if edge == 17:
                source = self.summed(array, z)
        elif edge >= 45:
            peer, source = "C", self.operand(array, edge - 45, 1 - self.core)
            target = (self.left_all, self.right_all)[edge - 45][array].at[1]
        else:
            kind, shard = (edge - 21) // 8, (edge - 21) % 8
            peer = ("Z1" if shard % 2 == 0 else "Z3", "Z1", "Z3")[kind]
            lanes = self.lanes(array, (z + (2, 1, 3)[kind]) % 4)
            source = self.totals[array].at[self.owner(*SHARD_ORDER[shard]), :, lanes]
            target = self.rounds.at[edge - 21]
        return pltpu.make_async_remote_copy(
            src_ref=source,
            dst_ref=target,
            send_sem=self.send_sem.at[array, edge],
            recv_sem=self.recv_sem.at[array, edge],
            device_id=self.ids[peer],
            device_id_type=MESH,
        )

    def wait_for(self, array, edge):
        z = self.z
        if edge < 11:
            landed = self.slot(array, edge)
        elif edge < 14:
            landed = self.quarters[array].at[edge - 11]
        elif edge < 17:
            landed = self.out_view(array, (z + 4 - (edge - 13)) % 4, self.core)
        elif edge < 21:
            landed = self.out_view(array, (z + edge - 17) % 4, 1 - self.core)
        elif edge >= 45:
            landed = (self.left_all, self.right_all)[edge - 45][array].at[1]
        else:
            landed = self.rounds.at[edge - 21]
        pltpu.make_async_remote_copy(
            src_ref=landed,
            dst_ref=landed,
            send_sem=self.send_sem.at[array, edge],
            recv_sem=self.recv_sem.at[array, edge],
            device_id=self.ids["C"],
            device_id_type=MESH,
        ).wait_recv()

    def receive(self, array, edge):
        self.wait_for(array, edge)
        peer, column, step, part, _ = REDUCE[edge]
        column, step = seen_by_receiver(peer, column, step)
        start, rows = part_rows(self.shapes[array], part)
        lanes = self.lanes(array, self.z)
        self.add(array, self.owner(column, step), start, rows, lanes, self.slot(array, edge))

    def receive_round(self, kind, shard):
        edge = 21 + 8 * kind + shard
        array = self.spread
        self.wait_for(array, edge)
        away = 0 if kind > 0 else (1 if shard % 2 == 0 else 3)
        rows = half_shape(self.shapes[array])[0]
        lanes = self.lanes(array, (self.z + away) % 4)
        self.add(
            array, self.owner(*SHARD_ORDER[shard]), 0, rows, lanes, self.rounds.at[edge - 21]
        )

    def stage(self, array, number):
        for edge in REDUCE_STAGES[number]:
            for earlier in REDUCE[edge][4]:
                self.receive(array, earlier)
            self.copy(array, edge).start()

    def operand(self, array, side, core):
        kind = self.shapes[array][2]
        if side == 0:
            return self.lefts[array].at[core] if kind == "rows" else self.lefts[array]
        right = self.rights[array]
        if kind == "rows":
            return right
        if len(right.shape) == 3:
            _, columns, _, _, offset = self.shapes[array]
            return right.at[core, :, pl.ds(offset, columns // 2)]
        return right.at[:, half_lanes(self.shapes[array], core)]

    def load(self, array, side):
        return pltpu.make_async_copy(
            self.operand(array, side, self.core),
            (self.left_all, self.right_all)[side][array].at[0],
            self.operand_sem.at[array, side],
        )

    def make(self, array, shards):
        columns = half_shape(self.shapes[array])[1]
        left, right, total = self.left_all[array], self.right_all[array], self.totals[array]
        for shard in shards:
            owner = self.owner(*SHARD_ORDER[shard])

            def chunk(lanes):
                if len(left.shape) == 3:
                    at = pl.ds(pl.multiple_of(owner * PADDED, PADDED), PADDED)
                    mine, other = left[0, :, at], left[1, :, at]
                else:
                    mine, other = left[0, owner], left[1, owner]
                total[owner, :, lanes] = (
                    dot_first(mine, right[0, :, lanes]) + dot_first(other, right[1, :, lanes])
                ).astype(jnp.bfloat16)

            if columns % 640 == 0 and columns > 640:

                @pl.loop(0, columns // 640)
                def _(index):
                    chunk(pl.ds(pl.multiple_of(index * 640, 128), 640))

            else:
                for first in range(0, columns, 512):
                    chunk(pl.ds(first, min(512, columns - first)))
            if self.extra is not None and array == 0:
                at = pl.ds(half_shape(self.shapes[array])[0] - 16, 16)
                total[owner, at, :128] += self.extra[owner]

    def store(self, array):
        return pltpu.make_async_copy(
            self.summed(array, self.z), self.out_view(array, self.z, self.core),
            self.local_sem.at[array],
        )

    def start_loads(self):
        for array in range(len(self.shapes)):
            for side in self.sides[array]:
                self.load(array, side).start()

    def start_exchange(self):
        for array in range(len(self.shapes)):
            for side in self.sides[array]:
                self.copy(array, 45 + side).start()

    def start(self):
        order = ([] if self.spread is None else [self.spread]) + self.plain
        for array in order:
            for side in self.sides[array]:
                self.load(array, side).wait()
                self.wait_for(array, 45 + side)
            if array == self.spread:
                self.make(array, range(SHARDS))
                for shard in range(SHARDS):
                    self.copy(array, 21 + shard).start()
            else:
                self.make(array, range(4))
                self.stage(array, 0)
        for array in self.plain:
            self.make(array, range(4, SHARDS))

    def first_round(self):
        for shard in range(SHARDS):
            self.receive_round(0, shard)
            self.copy(self.spread, 29 + shard).start()
            self.copy(self.spread, 37 + shard).start()

    def second_round(self, shards):
        for shard in shards:
            self.receive_round(1, shard)
            self.receive_round(2, shard)

    def end_plane(self, array):
        for edge in (8, 9, 10):
            self.receive(array, edge)
        for edge in (11, 12, 13) if array != self.spread else ():
            self.copy(array, edge).start()

    def end_z(self, array):
        if array != self.spread:
            start, rows, lanes = self.quarter(array, self.z)
            for edge in (11, 12, 13):
                self.wait_for(array, edge)
                self.add(
                    array, self.mine, start, rows, lanes, self.quarters[array].at[edge - 11]
                )
        for edge in (14, 15, 16, 17):
            self.copy(array, edge).start()
        self.store(array).start()

    def finish(self):
        for array in range(len(self.shapes)):
            for edge in (14, 15, 16):
                self.wait_for(array, edge)
                self.copy(array, 34 - edge).start()
        for array in range(len(self.shapes)):
            for edge in range(17, 21):
                self.wait_for(array, edge)
            for edge in range(REDUCE_EDGES):
                if edge >= 45:
                    started = edge - 45 in self.sides[array]
                elif array == self.spread:
                    started = edge not in (11, 12, 13)
                else:
                    started = edge < 21
                if started:
                    self.copy(array, edge).wait_send()
            self.store(array).wait()

    def steps(self):
        call = functools.partial
        steps = []
        if self.spread is not None:
            steps.append(self.first_round)
        steps += [call(self.stage, array, 1) for array in self.plain]
        if self.spread is not None:
            steps.append(call(self.second_round, range(4)))
            steps.append(call(self.stage, self.spread, 0))
            steps.append(call(self.second_round, range(4, SHARDS)))
            steps.append(call(self.stage, self.spread, 1))
        steps += [call(self.stage, array, 2) for array in self.plain]
        if self.spread is not None:
            steps.append(call(self.stage, self.spread, 2))
        steps += [call(self.end_plane, array) for array in self.plain]
        if self.spread is not None:
            steps.append(call(self.end_plane, self.spread))
            steps.append(call(self.end_z, self.spread))
        steps += [call(self.end_z, array) for array in self.plain]
        steps.append(self.finish)
        return steps


def reduce_kernel(shapes, *refs):
    count = len(shapes)
    lefts, rights, extra = refs[:count], refs[count : 2 * count], refs[2 * count]
    outs, scratch = refs[2 * count + 1 : 3 * count + 1], refs[3 * count + 1 :]
    reduce = Reduce(shapes, None, lefts, rights, extra, outs, scratch)
    reduce.start_loads()
    greet(reduce.ids, ("X", "Yp", "Ym", "C", "Z1", "Z2", "Z3"))
    reduce.start_exchange()
    reduce.start()
    for step in reduce.steps():
        step()


def reduce_gradients(lefts, rights, extra):
    count = len(ATTENTION)
    return pl.pallas_call(
        functools.partial(reduce_kernel, ATTENTION),
        name="reduce_gradients",
        out_shape=Reduce.out_shapes(ATTENTION),
        in_specs=[ANY] * (2 * count) + [VMEM],
        out_specs=[ANY] * count,
        scratch_shapes=Reduce.scratch(ATTENTION, None),
        compiler_params=pltpu.CompilerParams(
            collective_id=1, has_side_effects=True, vmem_limit_bytes=48 * 2**20
        ),
    )(*lefts, *rights, extra)


TOKENS = 1024
LOCAL = TOKENS // SHARDS
BLOCK = 256
NEGATIVE = -1e30


def two_groups(device):
    return (device == 1) | (device == 4)


def group_lanes(device, which):
    return pl.ds(pl.multiple_of(((2 * device) // 3 + which) * PAIR, PAIR), PAIR)


def pair_lanes(device):
    return pl.ds(pl.multiple_of(device * PAIR, PAIR), PAIR)


def token_rows(device):
    return pl.ds(pl.multiple_of(device * LOCAL, LOCAL), LOCAL)


def ring(me):
    return [(step, (me + step) % SHARDS, (me + SHARDS - step) % SHARDS) for step in range(1, SHARDS)]


def greet_all(me, others=()):
    barrier = pltpu.get_barrier_semaphore()
    ids = peer_ids()
    for device in [{"fsdp": target} for _, target, _ in ring(me)] + [ids[name] for name in others]:
        pl.semaphore_signal(barrier, inc=1, device_id=device, device_id_type=MESH)
    pl.semaphore_wait(barrier, SHARDS - 1 + len(others))


def turned(values):
    lane = lax.broadcasted_iota(jnp.int32, values.shape, 1)
    half = HEAD_WIDTH // 2
    ahead, behind = pltpu.roll(values, PAIR - half, 1), pltpu.roll(values, half, 1)
    return jnp.where(lane % HEAD_WIDTH < half, -ahead, behind)


def sent(source, target, send_sem, recv_sem, device):
    return pltpu.make_async_remote_copy(
        src_ref=source,
        dst_ref=target,
        send_sem=send_sem,
        recv_sem=recv_sem,
        device_id={"fsdp": device},
        device_id_type=MESH,
    )


def causal_mask(values):
    length = values.shape[1]
    row = lax.broadcasted_iota(jnp.int32, (BLOCK, BLOCK), 0)
    column = lax.broadcasted_iota(jnp.int32, (BLOCK, BLOCK), 1)
    own = jnp.where(column <= row, values[:, length - BLOCK :], NEGATIVE)
    if length == BLOCK:
        return own
    return jnp.concatenate([values[:, : length - BLOCK], own], 1)


def dot_t(left, right):
    return lax.dot_general(
        left, right, (((1,), (1,)), ((), ())), preferred_element_type=jnp.float32
    )


def dot_first(left, right):
    return lax.dot_general(
        left, right, (((0,), (0,)), ((), ())), preferred_element_type=jnp.float32
    )


def attend_kernel(with_gather, *refs):
    count = len(FEED_FORWARD) if with_gather else 0
    norm_ref, weight_ref, table_ref = refs[:3]
    mixed_ref, q_kept, kv_kept, lse_kept = refs[3 + count : 7 + count]
    q_ref, kv_ref, q_all, kv_all, lse_all, mixed_all, local_sem, send_sem, recv_sem = refs[
        7 + 2 * count : 16 + 2 * count
    ]
    background = None
    if with_gather:
        background = Gather(
            FEED_FORWARD, 0, refs[3 : 3 + count], refs[7 + count : 7 + 2 * count], refs[-3:]
        )
    me = lax.axis_index("fsdp")
    both = two_groups(me)
    second = jnp.where(both, 1, 0)

    def incoming(slot, step, device, sender):
        rows = token_rows(sender)
        return [
            sent(
                q_ref.at[slot, :, pair_lanes(device)], q_all.at[slot, rows, :],
                send_sem.at[0, slot, step], recv_sem.at[0, slot, step], device,
            ),
            sent(
                kv_ref.at[slot, :, group_lanes(device, 0)], kv_all.at[0, slot, rows, :],
                send_sem.at[1, slot, step], recv_sem.at[1, slot, step], device,
            ),
        ]

    def extra(slot, step, device, sender):
        group = jnp.where(two_groups(device), 1, 0)
        return sent(
            kv_ref.at[slot, :, group_lanes(device, group)], kv_all.at[1, slot, token_rows(sender), :],
            send_sem.at[2, slot, step], recv_sem.at[2, slot, step], device,
        )

    def outgoing(slot, step, device, sender):
        return sent(
            mixed_all.at[slot, token_rows(device), :], mixed_ref.at[slot, :, pair_lanes(sender)],
            send_sem.at[3, slot, step], recv_sem.at[3, slot, step], device,
        )

    def own_copies(slot):
        rows = token_rows(me)
        group = jnp.where(both, 1, 0)
        return [
            pltpu.make_async_copy(
                q_ref.at[slot, :, pair_lanes(me)], q_all.at[slot, rows, :], local_sem.at[0, slot]
            ),
            pltpu.make_async_copy(
                kv_ref.at[slot, :, group_lanes(me, 0)], kv_all.at[0, slot, rows, :],
                local_sem.at[1, slot],
            ),
            pltpu.make_async_copy(
                kv_ref.at[slot, :, group_lanes(me, group)], kv_all.at[1, slot, rows, :],
                local_sem.at[2, slot],
            ),
        ]

    def own_result(slot):
        return pltpu.make_async_copy(
            mixed_all.at[slot, token_rows(me), :], mixed_ref.at[slot, :, pair_lanes(me)],
            local_sem.at[3, slot],
        )

    greet_all(me, ("C", "Z1", "Z3") if background else ())
    pending = []
    if background:
        background.start()
        pending = background.steps()
    for first in range(0, WIDE, 2 * PAIR):
        width = min(2 * PAIR, WIDE - first)
        projected = jnp.dot(
            norm_ref[...], weight_ref[:, first : first + width], preferred_element_type=jnp.float32
        )
        for lane in range(first, first + width, PAIR):
            is_query = lane < FULL
            for slot in range(SLOTS):
                values = projected[
                    slot * LOCAL : (slot + 1) * LOCAL, lane - first : lane - first + PAIR
                ]
                cosine, sine = (table_ref[(0 if is_query else 2) + which, slot] for which in (0, 1))
                rotated = values * cosine + turned(values) * sine
                if is_query:
                    q_ref[slot, :, lane : lane + PAIR] = (rotated * HEAD_WIDTH ** (-0.5)).astype(
                        jnp.bfloat16
                    )
                else:
                    kv_ref[slot, :, lane - FULL : lane - FULL + PAIR] = rotated.astype(jnp.bfloat16)
    for slot in range(SLOTS):
        for step, target, _ in ring(me):
            for copy in incoming(slot, step, target, me):
                copy.start()

            @pl.when(two_groups(target))
            def _():
                extra(slot, step, target, me).start()

        for copy in own_copies(slot):
            copy.start()

    def do_pending(number):
        for _ in range(min(number, len(pending))):
            pending.pop(0)()

    def work(slot):
        for step, _, source in ring(me):
            for copy in incoming(slot, step, source, source):
                copy.wait_recv()

            @pl.when(both)
            def _():
                extra(slot, step, source, source).wait_recv()

        for copy in own_copies(slot):
            copy.wait()
        for block in range(TOKENS // BLOCK):
            rows = pl.ds(block * BLOCK, BLOCK)
            length = (block + 1) * BLOCK
            outs, totals = [], []
            for head in range(2):
                group = 0 if head == 0 else second
                lanes = slice(head * HEAD_WIDTH, (head + 1) * HEAD_WIDTH)
                query = q_all[slot, rows, lanes]
                keys = kv_all[group, slot, :length, :HEAD_WIDTH]
                values = kv_all[group, slot, :length, HEAD_WIDTH:]
                scores = causal_mask(dot_t(query, keys))
                highest = jnp.max(scores, -1, keepdims=True)
                weights = jnp.exp(scores - highest)
                total = jnp.sum(weights, -1, keepdims=True)
                out = jnp.dot(
                    weights.astype(jnp.bfloat16), values, preferred_element_type=jnp.float32
                )
                outs.append(out / total)
                totals.append(
                    jnp.broadcast_to(highest + jnp.log(total), (BLOCK, HEAD_WIDTH))
                )
            mixed_all[slot, rows, :] = jnp.concatenate(outs, 1).astype(jnp.bfloat16)
            lse_all[slot, rows, :] = jnp.concatenate(totals, 1)
        for step, target, _ in ring(me):
            outgoing(slot, step, target, me).start()
        own_result(slot).start()

    if background:
        do_pending(2)
        work(0)
        do_pending(3)
        work(1)
    else:
        pl.loop(0, SLOTS)(work)
    do_pending(len(pending))
    keep = [
        pltpu.make_async_copy(q_all, q_kept, local_sem.at[4, 0]),
        pltpu.make_async_copy(kv_all, kv_kept, local_sem.at[4, 1]),
        pltpu.make_async_copy(lse_all, lse_kept, local_sem.at[5, 0]),
    ]
    for copy in keep:
        copy.start()
    for slot in range(SLOTS):
        for step, target, source in ring(me):
            outgoing(slot, step, source, source).wait_recv()
            outgoing(slot, step, target, me).wait_send()
            for copy in incoming(slot, step, target, me):
                copy.wait_send()

            @pl.when(two_groups(target))
            def _():
                extra(slot, step, target, me).wait_send()

        own_result(slot).wait()
    for copy in keep:
        copy.wait()


Q_ALL = (SLOTS, TOKENS, PAIR)
KV_ALL = (2, SLOTS, TOKENS, PAIR)


def attend(norm, weight, tables, shards=()):
    bf16 = jnp.bfloat16
    with_gather = bool(shards)
    return pl.pallas_call(
        functools.partial(attend_kernel, with_gather),
        name="attend_gather" if with_gather else "attend",
        out_shape=[
            jax.ShapeDtypeStruct((SLOTS, LOCAL, FULL), bf16),
            jax.ShapeDtypeStruct(Q_ALL, bf16),
            jax.ShapeDtypeStruct(KV_ALL, bf16),
            jax.ShapeDtypeStruct(Q_ALL, jnp.float32),
        ]
        + (Gather.out_shapes(FEED_FORWARD) if with_gather else []),
        in_specs=[VMEM] * (3 + len(shards)),
        out_specs=[ANY] * (4 + len(shards)),
        scratch_shapes=[
            pltpu.VMEM((SLOTS, LOCAL, FULL), bf16),
            pltpu.VMEM((SLOTS, LOCAL, WIDE - FULL), bf16),
            pltpu.VMEM(Q_ALL, bf16),
            pltpu.VMEM(KV_ALL, bf16),
            pltpu.VMEM(Q_ALL, jnp.float32),
            pltpu.VMEM(Q_ALL, bf16),
            pltpu.SemaphoreType.DMA((6, SLOTS)),
            pltpu.SemaphoreType.DMA((4, SLOTS, SHARDS)),
            pltpu.SemaphoreType.DMA((4, SLOTS, SHARDS)),
        ]
        + (Gather.scratch(FEED_FORWARD, 0) if with_gather else []),
        compiler_params=pltpu.CompilerParams(
            collective_id=4 if with_gather else 2,
            has_side_effects=True,
            vmem_limit_bytes=40 * 2**20,
        ),
    )(norm, weight, tables, *shards)


def attend_back_kernel(with_reduce, *refs):
    count = len(FEED_FORWARD) if with_reduce else 0
    slope_ref, q_ref, kv_ref, lse_ref, weight_ref, table_ref = refs[:6]
    dqkv_ref, norm_slope_ref = refs[6 + 2 * count : 8 + 2 * count]
    scratch = refs[8 + 3 * count :]
    slope_all, q_all, kv_all, lse_all, dq_all, dkv_total, dkv_all = scratch[:7]
    dq_ref, dkv_ref, dkv_extra_ref, local_sem, send_sem, recv_sem = scratch[7:13]
    background = None
    if with_reduce:
        background = Reduce(
            FEED_FORWARD_BACK,
            REDUCE_SPREAD,
            refs[6 : 6 + count],
            refs[6 + count : 6 + 2 * count],
            None,
            refs[8 + 2 * count : 8 + 3 * count],
            scratch[13:],
        )
    me = lax.axis_index("fsdp")
    both = two_groups(me)
    second = jnp.where(both, 1, 0)
    extra_at = me // 4

    def incoming(slot, step, device, sender):
        return sent(
            slope_ref.at[slot, :, pair_lanes(device)], slope_all.at[slot, token_rows(sender), :],
            send_sem.at[0, slot, step], recv_sem.at[0, slot, step], device,
        )

    def outgoing(slot, step, device, sender):
        rows = token_rows(device)
        return [
            sent(
                dq_all.at[slot, rows, :], dq_ref.at[slot, :, pair_lanes(sender)],
                send_sem.at[1, slot, step], recv_sem.at[1, slot, step], device,
            ),
            sent(
                dkv_all.at[0, slot, rows, :], dkv_ref.at[sender, slot],
                send_sem.at[2, slot, step], recv_sem.at[2, slot, step], device,
            ),
        ]

    def extra(slot, step, device, sender):
        return sent(
            dkv_all.at[1, slot, token_rows(device), :], dkv_extra_ref.at[sender // 4, slot],
            send_sem.at[3, slot, step], recv_sem.at[3, slot, step], device,
        )

    def own_slope(slot):
        return pltpu.make_async_copy(
            slope_ref.at[slot, :, pair_lanes(me)], slope_all.at[slot, token_rows(me), :],
            local_sem.at[0, slot],
        )

    def own_results(slot):
        rows = token_rows(me)
        return [
            pltpu.make_async_copy(
                dq_all.at[slot, rows, :], dq_ref.at[slot, :, pair_lanes(me)], local_sem.at[1, slot]
            ),
            pltpu.make_async_copy(
                dkv_all.at[0, slot, rows, :], dkv_ref.at[me, slot], local_sem.at[2, slot]
            ),
        ]

    def own_extra(slot):
        return pltpu.make_async_copy(
            dkv_all.at[1, slot, token_rows(me), :], dkv_extra_ref.at[extra_at, slot],
            local_sem.at[3, slot],
        )

    loads = [
        pltpu.make_async_copy(q_ref, q_all, local_sem.at[4, 0]),
        pltpu.make_async_copy(kv_ref, kv_all, local_sem.at[4, 1]),
        pltpu.make_async_copy(lse_ref, lse_all, local_sem.at[5, 0]),
    ]
    for copy in loads:
        copy.start()
    if background:
        background.start_loads()
    greet_all(me, ("C", "Z1", "Z2", "Z3") if background else ())
    for slot in range(SLOTS):
        for step, target, _ in ring(me):
            incoming(slot, step, target, me).start()
        own_slope(slot).start()
    pending = []
    if background:
        background.start_exchange()
        background.start()
        pending = background.steps()
    for copy in loads:
        copy.wait()

    def work(slot):
        for step, _, source in ring(me):
            incoming(slot, step, source, source).wait_recv()
        own_slope(slot).wait()
        dkv_total[...] = jnp.zeros_like(dkv_total)
        for block in range(TOKENS // BLOCK):
            rows = pl.ds(block * BLOCK, BLOCK)
            length = (block + 1) * BLOCK
            outs = []
            for head in range(2):
                group = 0 if head == 0 else second
                lanes = slice(head * HEAD_WIDTH, (head + 1) * HEAD_WIDTH)
                query = q_all[slot, rows, lanes]
                slope = slope_all[slot, rows, lanes]
                lse = lse_all[slot, rows, head * HEAD_WIDTH : head * HEAD_WIDTH + 1]
                keys = kv_all[group, slot, :length, :HEAD_WIDTH]
                values = kv_all[group, slot, :length, HEAD_WIDTH:]
                probs = jnp.exp(causal_mask(dot_t(query, keys)) - lse)
                prob_slope = dot_t(slope, values)
                inner = jnp.sum(probs * prob_slope, -1, keepdims=True)
                score_slope = (probs * (prob_slope - inner)).astype(jnp.bfloat16)
                outs.append(
                    jnp.dot(score_slope, keys, preferred_element_type=jnp.float32)
                    * HEAD_WIDTH ** (-0.5)
                )
                dkv_total[group, :length, :] += jnp.concatenate(
                    [dot_first(score_slope, query), dot_first(probs.astype(jnp.bfloat16), slope)], 1
                )
            dq_all[slot, rows, :] = jnp.concatenate(outs, 1).astype(jnp.bfloat16)
        dkv_all[0, slot] = dkv_total[0].astype(jnp.bfloat16)
        dkv_all[1, slot] = dkv_total[1].astype(jnp.bfloat16)
        for step, target, _ in ring(me):
            for copy in outgoing(slot, step, target, me):
                copy.start()

            @pl.when(both)
            def _():
                extra(slot, step, target, me).start()

        for copy in own_results(slot):
            copy.start()

        @pl.when(both)
        def _():
            own_extra(slot).start()

    if background:
        work(0)
        for step in pending[:BACK_POINT]:
            step()
        work(1)
    else:
        pl.loop(0, SLOTS)(work)

    def collect():
        for slot in range(SLOTS):
            for step, _, source in ring(me):
                for copy in outgoing(slot, step, source, source):
                    copy.wait_recv()

                @pl.when(two_groups(source))
                def _():
                    extra(slot, step, source, source).wait_recv()

            for copy in own_results(slot):
                copy.wait()

            @pl.when(both)
            def _():
                own_extra(slot).wait()

            rows = pl.ds(slot * LOCAL, LOCAL)

            def reversed_rotation(values, table):
                return values * table_ref[table, slot] - turned(values * table_ref[table + 1, slot])

            for lane in range(0, FULL, PAIR):
                values = dq_ref[slot, :, lane : lane + PAIR].astype(jnp.float32)
                dqkv_ref[rows, lane : lane + PAIR] = reversed_rotation(values, 0).astype(
                    jnp.bfloat16
                )
            pairs = (
                (dkv_ref[0, slot], dkv_ref[1, slot]),
                (dkv_extra_ref[0, slot], dkv_ref[2, slot]),
                (dkv_ref[3, slot], dkv_ref[4, slot]),
                (dkv_extra_ref[1, slot], dkv_ref[5, slot]),
                (dkv_ref[6, slot], dkv_ref[7, slot]),
            )
            for group, (one, two) in enumerate(pairs):
                values = one.astype(jnp.float32) + two.astype(jnp.float32)
                lane = FULL + group * PAIR
                dqkv_ref[rows, lane : lane + PAIR] = reversed_rotation(values, 2).astype(
                    jnp.bfloat16
                )
        for first in range(0, FULL, 2 * PAIR):
            norm_slope_ref[:, first : first + 2 * PAIR] = dot_t(
                dqkv_ref[...], weight_ref[first : first + 2 * PAIR, :]
            )

    if background:
        for step in pending[BACK_POINT:BACK_COLLECT]:
            step()
        collect()
        for step in pending[BACK_COLLECT:]:
            step()
    else:
        collect()
    for slot in range(SLOTS):
        for step, target, source in ring(me):
            incoming(slot, step, target, me).wait_send()
            for copy in outgoing(slot, step, target, me):
                copy.wait_send()

            @pl.when(both)
            def _():
                extra(slot, step, target, me).wait_send()


REDUCE_SPREAD = 2
BACK_POINT = 3
BACK_COLLECT = 8


def attend_back(slope, kept, weight, tables, lefts=(), rights=()):
    bf16 = jnp.bfloat16
    with_reduce = bool(lefts)
    return pl.pallas_call(
        functools.partial(attend_back_kernel, with_reduce),
        name="attend_back_reduce" if with_reduce else "attend_back",
        out_shape=[
            jax.ShapeDtypeStruct((ROWS_HERE, WIDE), bf16),
            jax.ShapeDtypeStruct((ROWS_HERE, FULL), jnp.float32),
        ]
        + (Reduce.out_shapes(FEED_FORWARD) if with_reduce else []),
        in_specs=[ANY] * 4 + [VMEM] * 2 + [ANY] * (2 * len(lefts)),
        out_specs=[VMEM] * 2 + [ANY] * len(lefts),
        scratch_shapes=[
            pltpu.VMEM(Q_ALL, bf16),
            pltpu.VMEM(Q_ALL, bf16),
            pltpu.VMEM(KV_ALL, bf16),
            pltpu.VMEM(Q_ALL, jnp.float32),
            pltpu.VMEM(Q_ALL, bf16),
            pltpu.VMEM((2, TOKENS, PAIR), jnp.float32),
            pltpu.VMEM(KV_ALL, bf16),
            pltpu.VMEM((SLOTS, LOCAL, FULL), bf16),
            pltpu.VMEM((SHARDS, SLOTS, LOCAL, PAIR), bf16),
            pltpu.VMEM((2, SLOTS, LOCAL, PAIR), bf16),
            pltpu.SemaphoreType.DMA((6, SLOTS)),
            pltpu.SemaphoreType.DMA((4, SLOTS, SHARDS)),
            pltpu.SemaphoreType.DMA((4, SLOTS, SHARDS)),
        ]
        + (Reduce.scratch(FEED_FORWARD_BACK, REDUCE_SPREAD) if with_reduce else []),
        compiler_params=pltpu.CompilerParams(
            collective_id=5 if with_reduce else 3,
            has_side_effects=True,
            vmem_limit_bytes=(58 if with_reduce else 48) * 2**20,
        ),
    )(slope, *kept, weight, tables, *lefts, *rights)


FF_BLOCK = 512


def feed_back_kernel(slope_ref, down_ref, gate_w_ref, up_w_ref, gate_ref, up_ref, out_ref, norm_ref):
    slope = dot_t(slope_ref[...], down_ref[...])
    gate, up = gate_ref[...], up_ref[...]
    sigma = jax.nn.sigmoid(gate)
    gate_slope = (slope * up * sigma * (1.0 + gate * (1.0 - sigma))).astype(jnp.bfloat16)
    up_slope = (slope * gate * sigma).astype(jnp.bfloat16)
    out_ref[0] = gate_slope
    out_ref[1] = up_slope
    norm_slope = dot_t(gate_slope, gate_w_ref[...]) + dot_t(up_slope, up_w_ref[...])

    @pl.when(pl.program_id(0) == 0)
    def _():
        norm_ref[...] = norm_slope

    @pl.when(pl.program_id(0) > 0)
    def _():
        norm_ref[...] += norm_slope


def feed_back(down_in, down_weight, gate_up, gated):
    blocks = FF // FF_BLOCK
    tall = pl.BlockSpec((ROWS_HERE, MODEL), lambda i: (0, 0))
    return pl.pallas_call(
        feed_back_kernel,
        name="feed_back",
        grid=(blocks,),
        out_shape=[
            jax.ShapeDtypeStruct((2, ROWS_HERE, FF), jnp.bfloat16),
            jax.ShapeDtypeStruct((ROWS_HERE, MODEL), jnp.float32),
        ],
        in_specs=[
            tall,
            pl.BlockSpec((FF_BLOCK, MODEL), lambda i: (i, 0)),
            pl.BlockSpec((MODEL, FF_BLOCK), lambda i: (0, i)),
            pl.BlockSpec((MODEL, FF_BLOCK), lambda i: (0, i + blocks)),
            pl.BlockSpec((ROWS_HERE, FF_BLOCK), lambda i: (0, i)),
            pl.BlockSpec((ROWS_HERE, FF_BLOCK), lambda i: (0, i + blocks)),
        ],
        out_specs=[pl.BlockSpec((2, ROWS_HERE, FF_BLOCK), lambda i: (0, 0, i)), tall],
        compiler_params=pltpu.CompilerParams(vmem_limit_bytes=40 * 2**20),
    )(down_in, down_weight, gate_up, gate_up, gated, gated)


def finish_kernel(
    flags_ref, hidden_slope_ref, values_ref, slope_ref, gain_ref, result_ref,
    grads_ref, outputs_ref, gain_slope_ref,
):
    swapped, first = flags_ref[0], flags_ref[1]
    slopes, gain_slope = norm_backward(values_ref[...], gain_ref[...], slope_ref[...])
    slopes += hidden_slope_ref[...]
    low = slopes.astype(jnp.bfloat16).astype(jnp.float32)
    slopes = jnp.where(first == 1, slopes, low)
    gain_slope_ref[...] = gain_slope.reshape(1, MODEL)
    for slot in range(SLOTS):
        place = jnp.where(swapped == 1, 1 - slot, slot)
        rows = slice(slot * LOCAL, (slot + 1) * LOCAL)
        for shard in range(SHARDS):
            into = slice(shard * ROWS, (shard + 1) * ROWS)
            have = slice(shard * PADDED, shard * PADDED + ROWS)
            grads_ref[place, :, into] = slopes[rows, have]
            outputs_ref[slot, :, into] = result_ref[rows, have]


def finish(flags, hidden_slope, values, slope, gain, result):
    return pl.pallas_call(
        finish_kernel,
        name="finish",
        out_shape=[
            jax.ShapeDtypeStruct((SLOTS, LOCAL, D), jnp.float32),
            jax.ShapeDtypeStruct((SLOTS, LOCAL, D), jnp.bfloat16),
            jax.ShapeDtypeStruct((1, MODEL), jnp.float32),
        ],
        in_specs=[pl.BlockSpec(memory_space=pltpu.SMEM)] + [VMEM] * 5,
        out_specs=[VMEM] * 3,
        compiler_params=pltpu.CompilerParams(vmem_limit_bytes=40 * 2**20),
    )(flags, hidden_slope, values, slope, gain, result)


def rotary_tables(positions):
    half = HEAD_WIDTH // 2
    frequency = BASE ** (-(jnp.arange(half).astype(jnp.float32) * (2.0 / HEAD_WIDTH)))
    angle = positions.astype(jnp.float32)[..., None] * frequency
    cosine, sine = jnp.cos(angle), jnp.sin(angle)
    one, zero = jnp.ones_like(cosine), jnp.zeros_like(sine)
    return jnp.stack(
        [
            jnp.concatenate(parts, -1)
            for parts in (
                [cosine] * 4,
                [sine] * 4,
                [cosine, cosine, one, one],
                [sine, sine, zero, zero],
            )
        ]
    )


def widened(values):
    lead = values.shape[:-1]
    split = values[..., QUERY_WIDTH:].reshape(lead + (2, KEY_VALUE_HEADS, HEAD_WIDTH))
    return jnp.concatenate(
        [
            values[..., :QUERY_WIDTH],
            jnp.zeros(lead + (FULL - QUERY_WIDTH,), values.dtype),
            jnp.swapaxes(split, -2, -3).reshape(lead + (2 * KEY_WIDTH,)),
        ],
        -1,
    )


def narrowed(values):
    lead = values.shape[:-1]
    split = values[..., FULL:].reshape(lead + (KEY_VALUE_HEADS, 2, HEAD_WIDTH))
    return jnp.concatenate(
        [values[..., :QUERY_WIDTH], jnp.swapaxes(split, -2, -3).reshape(lead + (2 * KEY_WIDTH,))],
        -1,
    )


def mean(values):
    return jnp.sum(values, -1, keepdims=True) * (1.0 / D)


def normed(values, gain):
    return values * lax.rsqrt(mean(values * values) + EPSILON) * gain


def norm_backward(values, gain, upstream):
    row_scale = lax.rsqrt(mean(values * values) + EPSILON)
    unit = values * row_scale
    gain_slope = jnp.sum(upstream * unit, 0)
    inner = upstream * gain
    return (row_scale * (inner - unit * mean(inner * unit)), gain_slope)


def padded(values):
    split = values.reshape(values.shape[:-1] + (SHARDS, ROWS))
    widths = ((0, 0),) * (split.ndim - 1) + ((0, PADDED - ROWS),)
    return jnp.pad(split, widths).reshape(values.shape[:-1] + (MODEL,))


def unpadded(values):
    split = values.reshape(values.shape[:-1] + (SHARDS, PADDED))
    return split[..., :ROWS].reshape(values.shape[:-1] + (D,))


def forward_layer(layer_in, tables, weights, shards=()):
    attend_in, attend_out, gate_up, down_weight, gains = weights
    rows = ROWS_HERE
    values = layer_in.reshape(rows, MODEL).astype(jnp.float32)
    first_norm = normed(values, gains[0]).astype(jnp.bfloat16)
    mixed, *attended = attend(first_norm, attend_in, tables, shards)
    if shards:
        *attended, gate_up, down_weight = attended
        gate_up = gate_up.reshape(-1, 2 * FF)
        down_weight = down_weight.reshape(-1, MODEL)
    mixed = mixed.reshape(rows, FULL)
    hidden = values + jnp.dot(mixed, attend_out, preferred_element_type=jnp.float32)
    second_norm = normed(hidden, gains[1]).astype(jnp.bfloat16)
    gated = jnp.dot(second_norm, gate_up, preferred_element_type=jnp.float32)
    act = (jax.nn.silu(gated[:, :FF]) * gated[:, FF:]).astype(jnp.bfloat16)
    result = hidden + jnp.dot(act, down_weight, preferred_element_type=jnp.float32)
    kept = (
        values,
        first_norm,
        attended,
        mixed,
        hidden,
        second_norm,
        gated,
        act,
    )
    weights = (attend_in, attend_out, gate_up, down_weight, gains)
    return (result.astype(jnp.bfloat16).reshape(layer_in.shape), kept, weights)


def backward_layer(upstream, kept, tables, weights, ending=None):
    last = ending is not None
    attend_in, attend_out, gate_up, down_weight, gains = weights
    (
        values,
        first_norm,
        attended,
        mixed,
        hidden,
        second_norm,
        gated,
        act,
    ) = kept
    batches, local_count = upstream.shape[:2]
    rows = batches * local_count
    down_in = upstream.reshape(rows, MODEL)
    upstream = down_in.astype(jnp.float32)
    gated_slope, second_slope = feed_back(down_in, down_weight, gate_up, gated)
    hidden_part, second_gain = norm_backward(hidden, gains[1], second_slope)
    hidden_slope = upstream + hidden_part
    branch_slope = hidden_slope.astype(jnp.bfloat16)
    mixed_gradient = jnp.einsum(
        "td,qd->tq", branch_slope, attend_out, preferred_element_type=jnp.float32
    ).astype(jnp.bfloat16)
    lefts, rights = (), ()
    if last:
        lefts = (second_norm, by_shard(act))
        rights = (gated_slope, down_in)
    projected_slope, first_slope, *summed = attend_back(
        mixed_gradient.reshape(batches, local_count, FULL),
        attended,
        attend_in,
        tables,
        lefts,
        rights,
    )
    if not last:
        input_part, _ = norm_backward(values, gains[0], first_slope)
        return (hidden_slope + input_part).reshape(batches, local_count, MODEL)
    flags, result = ending
    input_grads, outputs, first_gain = finish(
        flags, hidden_slope, values, first_slope, gains[:1], result.reshape(rows, MODEL)
    )
    gain_slopes = jnp.stack([first_gain[0], second_gain])
    lefts = (by_core(first_norm), by_core(padded(mixed[:, :QUERY_WIDTH])))
    rights = (projected_slope, branch_slope)
    summed = (*reduce_gradients(lefts, rights, spare_rows(gain_slopes)), *summed)
    return (input_grads, outputs, summed)


def passed_along(value, steps):
    return lax.ppermute(value, "section", [(0, 1)] if steps > 0 else [(1, 0)])


def with_other_core(value):
    size = lax.axis_size("dp")
    other = lax.ppermute(value, "dp", [(index, index ^ 1) for index in range(size)])
    return other


def by_shard(values):
    return values.reshape(ROWS_HERE, SHARDS, -1).swapaxes(0, 1)


def by_core(values):
    return values.reshape(ROWS_HERE, SHARDS, 2, -1).transpose(2, 1, 0, 3)


def spare_rows(gain_slopes):
    core = lax.axis_index("dp") % 2
    gains = (gain_slopes + with_other_core(gain_slopes)).reshape(2, SHARDS, PADDED).swapaxes(0, 1)
    gains = jnp.where(core == 1, gains, 0.0).astype(jnp.bfloat16)
    return jnp.pad(gains, ((0, 0), (8, 6), (0, 0)))


def body(
    inputs, positions, plan, attend_in, attend_out, gate_up, down_weight, norm_gains, cotangent
):
    section_index = lax.axis_index("section")
    extra = PADDED - ROWS
    in_shard = jnp.concatenate(
        [
            widened(attend_in[0]),
            jnp.pad(norm_gains[0], ((0, extra - 2), (0, WIDE - ROWS))),
        ],
        0,
    )
    gathered = gather_weights((in_shard, jnp.pad(padded(attend_out[0]), ((0, extra), (0, 0)))))
    gains = gathered[0][:, ROWS : ROWS + 2, :PADDED].swapaxes(0, 1).reshape(2, MODEL)
    out_weight = gathered[1][:, :ROWS].reshape(QUERY_WIDTH, MODEL)
    weights = (
        gathered[0].reshape(-1, WIDE),
        jnp.pad(out_weight, ((0, FULL - QUERY_WIDTH), (0, 0))),
        None,
        None,
        gains.astype(jnp.float32),
    )
    shards = (
        jnp.pad(gate_up[0], ((0, extra), (0, 0))),
        padded(down_weight[0]),
    )
    plan_row = plan[0]
    swap = plan_row[0] == 1

    def in_slots(values):
        return jnp.where(swap, values[::-1, 0], values[:, 0])

    fresh = padded(in_slots(inputs))
    tables = rotary_tables(in_slots(positions))
    given = padded(cotangent[:, 0])
    result, _, weights = forward_layer(fresh, tables, weights, shards)
    layer_in = jnp.where(section_index == 0, fresh, passed_along(result, 1))
    outputs, kept, _ = forward_layer(layer_in, tables, weights)
    input_slope = backward_layer(given, kept, tables, weights)
    back = passed_along(input_slope.astype(jnp.bfloat16), -1)
    upstream = jnp.where(section_index == 1, given, back)
    flags = jnp.stack([swap, section_index == 0]).astype(jnp.int32)
    input_slopes, outputs, summed = backward_layer(
        upstream, kept, tables, weights, (flags, outputs)
    )
    full = [value.astype(jnp.float32) for value in summed]
    return (
        outputs[None, :, None],
        input_slopes[None, :, None],
        narrowed(full[0])[None, :ROWS],
        unpadded(full[1][:ROWS])[None],
        full[2][None, :ROWS],
        unpadded(full[3])[None],
        full[0][None, ROWS : ROWS + 2, :ROWS],
    )


def solution(mesh):
    in_specs = (
        P(None, "dp", "fsdp", None),
        P(None, "dp", "fsdp"),
        P("dp", None),
        P("section", "fsdp", None),
        P("section", "fsdp", None),
        P("section", "fsdp", None),
        P("section", "fsdp", None),
        P("section", None, "fsdp"),
        P(None, "dp", "fsdp", None),
    )
    out_specs = (
        P("section", None, "dp", "fsdp", None),
        P("section", None, "dp", "fsdp", None),
        P("section", "fsdp", None),
        P("section", "fsdp", None),
        P("section", "fsdp", None),
        P("section", "fsdp", None),
        P("section", None, "fsdp"),
    )
    return jax.shard_map(body, mesh=mesh, in_specs=in_specs, out_specs=out_specs, check_vma=False)
```

profile of v0, /device:TPU:1, one launch (start us, length us, event | category | flops | bytes accessed | tf_op | source)
XLA Modules:
  0.0 443.7 jit_solution(17151270601627416987)
XLA Ops:
  9.6 28.7 %gather_weights.1 = (bf16[8,128,1664]{2,1,0:T(8,128)(2,1)}, bf16[8,128,1024]{2,1,0:T(8,128)(2,1)}) custom-call(bf16[128,1664]{1,0:T(8,128)(2,1)} %fusion.41.refs_0_, bf16[128,1024]{1,0:T(8,128)(2,1)} %pad.43.refs_1_), custom_call_target="tpu_custom_call" | custom-call | tf_op jit(solution)/shard_map/gather_weights/pallas_call | solution.py:286
  38.3 3.2 slice.80
  41.7 2.5 pad.44.refs_3_
  44.2 2.8 reshape_squeeze.11
  49.7 65.8 %attend_gather.1 = (bf16[2,128,1024]{2,1,0:T(8,128)(2,1)S(1)}, bf16[2,1024,128]{2,1,0:T(8,128)(2,1)}, bf16[2,2,1024,128]{3,2,1,0:T(8,128)(2,1)}, f32[2,1024,128]...) custom-call(bf16[256,1024]{1,0:T(8,128)(2,1)S(1)} %fusion.33.refs_0_, ...), custom_call_target="tpu_custom_call" | custom-call | tf_op jit(solution)/shard_map/attend_gather/pallas_call | solution.py:949
  116.9 5.8 %fusion.37 = f32[256,5120]{1,0:T(8,128)S(1)} fusion(bf16[1024,5120]{1,0:T(8,128)(2,1)} %bitcast.152, f32[256,1024]{1,0:T(8,128)S(1)} %get-tuple-element.82, f32[1024]{0:T(1024)S(1)} %bitcast.185, f32[256]{0:T(256)S(1)} %add_rsqrt_fusion.1), kind=kOutput, calls=%fused_computation.50 | convolution fusion | flops 2685140992 | bytes 16782336 | tf_op jit(solution)/shard_map/dot_general | solution.py:1396
  122.8 2.5 fusion.28
  125.2 2.0 copy.29
  127.2 5.4 %collective-permute-start = (bf16[2,128,1024]{1,0,2:T(2,128)(2,1)}, bf16[2,128,1024]{1,0,2:T(2,128)(2,1)}, u32[]{:S(2)}, u32[]{:S(2)}) collective-permute-start(bf16[2,128,1024]{1,0,2:T(2,128)(2,1)} %copy.29), channel_id=1, source_target_pairs={{0,64},{1,65},{2,66},{3,67},{4,68},{5,69},{6,70},{7,71},{8,72},{9,... | collective-permute-start | bytes 1572872 | tf_op jit(solution)/shard_map/ppermute | solution.py:1464
  132.7 2.3 copy.61
  135.0 2.1 copy.23
  137.1 1.9 pad.39
  139.0 2.1 reshape.207
  141.1 2.0 copy.63
  143.1 2.2 pad.40.clone
  145.4 3.0 multiply_reduce_fusion.5
  148.5 2.3 copy.30
  150.8 3.0 reshape.231
  156.3 38.0 %attend.1 = (bf16[2,128,1024]{2,1,0:T(8,128)(2,1)S(1)}, bf16[2,1024,128]{2,1,0:T(8,128)(2,1)S(1)}, bf16[2,2,1024,128]{3,2,1,0:T(8,128)(2,1)S(1)}, f32[2,1024,128]{2,1,0:T(8,128)S(1)}) custom-call(bf16[256,1024]{1,0:T(8,128)(2,1)S(1)} %multiply_convert_fusion.2.refs_0_, bf16[1024,1664]{1,0:T(8,128)(2,1)S(1)} %bitcast.128, f32[4,2,128,128]{3,2,1,0:T(8,128)S(1)} %copy-done.4), custom_call_target="tpu_custom_call" | custom-call | tf_op jit(solution)/shard_map/attend/pallas_call | solution.py:949
  195.3 6.4 %fusion.55.gate_ref.up_ref = f32[256,5120]{1,0:T(8,128)S(1)} fusion(bf16[256,1024]{1,0:T(8,128)(2,1)S(1)} %multiply_convert_fusion.1.refs_6_, bf16[1024,5120]{1,0:T(8,128)(2,1)} %bitcast.153), kind=kOutput, calls=%fused_computation.96 | convolution fusion | flops 2684354560 | bytes 16252928 | tf_op jit(solution)/shard_map/dot_general | solution.py:1396
  204.1 11.2 %feed_back.2 = (bf16[2,256,2560]{2,1,0:T(8,128)(2,1)}, f32[256,1024]{1,0:T(8,128)S(1)}) custom-call(bf16[256,1024]{1,0:T(8,128)(2,1)S(1)} %bitcast.145, bf16[2560,1024]{1,0:T(8,128)(2,1)S(1)} %bitcast.137, bf16[1024,5120]{1,0:T(8,128)(2,1)} %bitcast.154, bf16[1024,5120]{1,0:T(8,128)(2,1)} %bitcast.155, f32[256,5120]{1,0:T(8,128)} %copy-done.21, ...), custom_call_target="tpu_custom_call" | custom-call | tf_op jit(solution)/shard_map/feed_back/pallas_call | solution.py:1259
  216.7 32.9 %attend_back.1 = (bf16[256,1664]{1,0:T(8,128)(2,1)}, f32[256,1024]{1,0:T(8,128)S(1)}) custom-call(bf16[2,128,1024]{2,1,0:T(8,128)(2,1)S(1)} %bitcast.148, bf16[2,1024,128]{2,1,0:T(8,128)(2,1)S(1)} %get-tuple-element.36.refs_1_, bf16[2,2,1024,128]{3,2,1,0:T(8,128)(2,1)S(1)} %get-tuple-element.37.refs_2_, f32[2,1024,128]{2,1,0:T(8,128)S(1)} %get-tuple-element.38.refs_3_, ...), custom_call_target="tpu_custom_call" | custom-call | tf_op jit(solution)/shard_map/attend_back/pallas_call | solution.py:1200
  254.9 1.9 copy.33
  257.6 2.1 fusion.31.refs_0_
  259.7 4.8 %fusion.21.result_ref = bf16[256,1024]{1,0:T(8,128)(2,1)S(1)} fusion(f32[256,1024]{1,0:T(8,128)} %copy-done.22, bf16[256,2560]{1,0:T(8,128)(2,1)} %copy-done.30, bf16[2560,1024]{1,0:T(8,128)(2,1)} %bitcast.131), kind=kOutput, calls=%fused_computation.18 | convolution fusion | flops 1342701568 | bytes 8126464 | tf_op jit(solution)/shard_map/dot_general | solution.py:1398
  265.7 9.9 %feed_back.3 = (bf16[2,256,2560]{2,1,0:T(8,128)(2,1)S(1)}, f32[256,1024]{1,0:T(8,128)S(1)}) custom-call(bf16[256,1024]{1,0:T(8,128)(2,1)S(1)} %bitcast.141, bf16[2560,1024]{1,0:T(8,128)(2,1)S(1)} %bitcast.140, bf16[1024,5120]{1,0:T(8,128)(2,1)} %bitcast.156, bf16[1024,5120]{1,0:T(8,128)(2,1)} %bitcast.157, f32[256,5120]{1,0:T(8,128)} %copy-done.21, ...), custom_call_target="tpu_custom_call" | custom-call | tf_op jit(solution)/shard_map/feed_back/pallas_call | solution.py:1259
  279.6 105.7 %attend_back_reduce.1 = (bf16[256,1664]{1,0:T(8,128)(2,1)}, f32[256,1024]{1,0:T(8,128)}, bf16[128,5120]{1,0:T(8,128)(2,1)}, bf16[320,1024]{1,0:T(8,128)(2,1)}) custom-call(bf16[2,128,1024]{2,1,0:T(8,128)(2,1)} %bitcast.183, bf16[2,1024,128]{2,1,0:T(8,128)(2,1)} %copy-done.12, bf16[2,2,1024,128]{3,2,1,0:T(8,128)(2,1)} %copy-done.8, ...), custom_call_target="tpu_custom_call" | custom-call | tf_op jit(solution)/shard_map/attend_back_reduce/pallas_call | solution.py:1200
  388.2 1.7 bitcast_convert_fusion
  391.2 2.1 copy.40
  393.3 2.5 copy.41
  395.8 2.8 reshape.234
  398.6 40.5 %reduce_gradients.1 = (bf16[128,1664]{1,0:T(8,128)(2,1)S(1)}, bf16[128,1024]{1,0:T(8,128)(2,1)S(1)}) custom-call(bf16[2,8,256,64]{3,2,1,0:T(8,128)(2,1)S(1)} %fusion.31.refs_0_, bf16[2,8,256,64]{3,2,1,0:T(8,128)(2,1)S(1)} %bitcast.143, bf16[256,1664]{1,0:T(8,128)(2,1)S(1)} %copy-done.17, bf16[256,1024]{1,0:T(8,128)(2,1)S(1)} %get-tuple-element.67.refs_3_, ...), custom_call_target="tpu_custom_call" | custom-call | tf_op jit(solution)/shard_map/reduce_gradients/pallas_call | solution.py:681
  (174 shorter events, 39.1 us)
Async XLA Ops:
  1.6 5.9 %copy-start.36 = (bf16[1,120,960]{2,1,0:T(8,128)(2,1)S(1)}, bf16[1,120,960]{2,1,0:T(8,128)(2,1)}, u32[]{:S(2)}) copy-start(bf16[1,120,960]{2,1,0:T(8,128)(2,1)} %param.13) | copy-start | bytes 691204
  5.0 3.8 copy-start.29
  5.0 3.8 copy-start.38
  8.8 32.7 %copy-start.37 = (s32[2,1,128]{2,1,0:T(1,128)S(1)}, s32[2,1,128]{2,1,0:T(1,128)}, u32[]{:S(2)}) copy-start(s32[2,1,128]{2,1,0:T(1,128)} %param.10) | copy-start | bytes 3076
  49.6 65.9 %copy-start.3 = (f32[4,2,128,128]{3,2,1,0:T(8,128)}, f32[4,2,128,128]{3,2,1,0:T(8,128)S(1)}, u32[]{:S(2)}) copy-start(f32[4,2,128,128]{3,2,1,0:T(8,128)S(1)} %pad_maximum_fusion.1.refs_2_.refs_5_) | copy-start | bytes 1572868
  49.7 65.8 %copy-start.24 = (bf16[8,120,1024]{2,1,0:T(8,128)(2,1)S(1)}, bf16[8,120,1024]{2,1,0:T(8,128)(2,1)}, u32[]{:S(2)}) copy-start(bf16[8,120,1024]{2,1,0:T(8,128)(2,1)} %slice.80) | copy-start | bytes 5898244
  115.5 7.2 %slice-start = ((s8[5242880]{0:T(1024)(128)(4,1)}), s8[4194304]{0:T(1024)(128)(4,1)S(1)}, s32[]{:S(2)}) async-start(s8[5242880]{0:T(1024)(128)(4,1)} %bitcast.132), calls=%async_computation | async-start | bytes 8388608
  116.9 5.8 %slice-start.1 = ((s8[5242880]{0:T(1024)(128)(4,1)}), s8[1048576]{0:T(1024)(128)(4,1)S(1)}, s32[]{:S(2)}) async-start(s8[5242880]{0:T(1024)(128)(4,1)} %bitcast.132), calls=%async_computation.1 | async-start | bytes 2097152
  127.2 18.2 %collective-permute-start = (bf16[2,128,1024]{1,0,2:T(2,128)(2,1)}, bf16[2,128,1024]{1,0,2:T(2,128)(2,1)}, u32[]{:S(2)}, u32[]{:S(2)}) collective-permute-start(bf16[2,128,1024]{1,0,2:T(2,128)(2,1)} %copy.29), channel_id=1, source_target_pairs={{0,64},{1,65},{2,66},{3,67},{4,68},{5,69},{6,70},{7,71},{8,72},{9,... | collective-permute-start | bytes 1572872 | tf_op jit(solution)/shard_map/ppermute | solution.py:1464
  156.2 38.1 %copy-start.1 = (f32[2,128,1024]{2,1,0:T(8,128)S(1)}, f32[2,128,1024]{2,1,0:T(8,128)}, u32[]{:S(2)}) copy-start(f32[2,128,1024]{2,1,0:T(8,128)} %copy.30) | copy-start | bytes 3145732
  156.2 38.1 %copy-start.25 = (bf16[8,120,1024]{2,1,0:T(8,128)(2,1)S(1)}, bf16[8,120,1024]{2,1,0:T(8,128)(2,1)}, u32[]{:S(2)}) copy-start(bf16[8,120,1024]{2,1,0:T(8,128)(2,1)} %slice.80) | copy-start | bytes 5898244
  194.3 22.2 %copy-start.8 = (bf16[2,2,1024,128]{3,2,1,0:T(8,128)(2,1)}, bf16[2,2,1024,128]{3,2,1,0:T(8,128)(2,1)S(1)}, u32[]{:S(2)}) copy-start(bf16[2,2,1024,128]{3,2,1,0:T(8,128)(2,1)S(1)} %get-tuple-element.37.refs_2_) | copy-start | bytes 3145732
  194.3 22.2 %copy-start.9 = (f32[2,1024,128]{2,1,0:T(8,128)}, f32[2,1024,128]{2,1,0:T(8,128)S(1)}, u32[]{:S(2)}) copy-start(f32[2,1024,128]{2,1,0:T(8,128)S(1)} %get-tuple-element.38.refs_3_) | copy-start | bytes 3145732
  194.3 22.2 %copy-start.12 = (bf16[2,1024,128]{2,1,0:T(8,128)(2,1)}, bf16[2,1024,128]{2,1,0:T(8,128)(2,1)S(1)}, u32[]{:S(2)}) copy-start(bf16[2,1024,128]{2,1,0:T(8,128)(2,1)S(1)} %get-tuple-element.36.refs_1_) | copy-start | bytes 1572868
  195.1 54.7 %copy-start.22 = (f32[256,1024]{1,0:T(8,128)}, f32[256,1024]{1,0:T(8,128)S(1)}, u32[]{:S(2)}) copy-start(f32[256,1024]{1,0:T(8,128)S(1)} %get-tuple-element.84) | copy-start | bytes 3145732
  195.1 8.9 %slice-start.2 = ((s8[5242880]{0:T(1024)(128)(4,1)}), s8[4194304]{0:T(1024)(128)(4,1)S(1)}, s32[]{:S(2)}) async-start(s8[5242880]{0:T(1024)(128)(4,1)} %bitcast.135), calls=%async_computation.2 | async-start | bytes 8388608
  195.3 6.5 %copy-start.31 = (bf16[256,1024]{1,0:T(8,128)(2,1)}, bf16[256,1024]{1,0:T(8,128)(2,1)S(1)}, u32[]{:S(2)}) copy-start(bf16[256,1024]{1,0:T(8,128)(2,1)S(1)} %multiply_convert_fusion.1.refs_6_) | copy-start | bytes 1572868
  195.3 8.8 %slice-start.3 = ((s8[5242880]{0:T(1024)(128)(4,1)}), s8[1048576]{0:T(1024)(128)(4,1)S(1)}, s32[]{:S(2)}) async-start(s8[5242880]{0:T(1024)(128)(4,1)} %bitcast.135), calls=%async_computation.3 | async-start | bytes 2097152
  204.1 48.3 %copy-start.30 = (bf16[256,2560]{1,0:T(8,128)(2,1)}, bf16[256,2560]{1,0:T(8,128)(2,1)S(1)}, u32[]{:S(2)}) copy-start(bf16[256,2560]{1,0:T(8,128)(2,1)S(1)} %fusion) | copy-start | bytes 3932164
  204.1 11.5 %copy-start.27 = (bf16[2,128,8,128]{3,2,1,0:T(8,128)(2,1)S(1)}, bf16[2,128,8,128]{3,2,1,0:T(8,128)(2,1)}, u32[]{:S(2)}) copy-start(bf16[2,128,8,128]{3,2,1,0:T(8,128)(2,1)} %pad.39) | copy-start | bytes 1572868
  251.1 13.4 %collective-permute-start.1 = (bf16[2,128,1024]{2,1,0:T(8,128)(2,1)}, bf16[2,128,1024]{2,1,0:T(8,128)(2,1)}, u32[]{:S(2)}, u32[]{:S(2)}) collective-permute-start(bf16[2,128,1024]{2,1,0:T(8,128)(2,1)} %bitcast.31), channel_id=1, source_target_pairs={{64,0},{65,1},{66,2},{67,3},{68,4},{69,5},{70,6},{71,7},{72,8},{73... | collective-permute-start | bytes 1572872 | tf_op jit(solution)/shard_map/ppermute | solution.py:1464
  253.3 3.6 copy-start.14
  257.6 8.1 %slice-start.4 = ((s8[5242880]{0:T(1024)(128)(4,1)}), s8[4194304]{0:T(1024)(128)(4,1)S(1)}, s32[]{:S(2)}) async-start(s8[5242880]{0:T(1024)(128)(4,1)} %bitcast.138), calls=%async_computation.4 | async-start | bytes 8388608
  259.7 4.8 %copy-start.33 = (bf16[2,128,1024]{2,1,0:T(8,128)(2,1)S(1)}, bf16[2,128,1024]{2,1,0:T(8,128)(2,1)}, u32[]{:S(2)}) copy-start(bf16[2,128,1024]{2,1,0:T(8,128)(2,1)} %reshape.207) | copy-start | bytes 1572868
  259.7 6.0 %slice-start.5 = ((s8[5242880]{0:T(1024)(128)(4,1)}), s8[1048576]{0:T(1024)(128)(4,1)S(1)}, s32[]{:S(2)}) async-start(s8[5242880]{0:T(1024)(128)(4,1)} %bitcast.138), calls=%async_computation.5 | async-start | bytes 2097152
  265.6 10.3 %copy-start.6 = (bf16[2,128,1024]{2,1,0:T(8,128)(2,1)}, bf16[2,128,1024]{2,1,0:T(8,128)(2,1)S(1)}, u32[]{:S(2)}) copy-start(bf16[2,128,1024]{2,1,0:T(8,128)(2,1)S(1)} %broadcast_select_fusion.1) | copy-start | bytes 1572868
  265.7 9.9 %copy-start.23 = (f32[256,1024]{1,0:T(8,128)S(1)}, f32[256,1024]{1,0:T(8,128)}, u32[]{:S(2)}) copy-start(f32[256,1024]{1,0:T(8,128)} %copy-done.22) | copy-start | bytes 3145732
  279.6 105.7 %copy-start.2 = (f32[2,128,1024]{2,1,0:T(8,128)S(1)}, f32[2,128,1024]{2,1,0:T(8,128)}, u32[]{:S(2)}) copy-start(f32[2,128,1024]{2,1,0:T(8,128)} %copy.30) | copy-start | bytes 3145732
  387.9 3.2 copy-start.16
  387.9 3.2 copy-start.18
  388.0 10.6 %collective-permute-start.2 = (f32[2,1024]{1,0:T(2,128)S(1)}, f32[2,1024]{1,0:T(2,128)S(1)}, u32[]{:S(2)}, u32[]{:S(2)}) collective-permute-start(f32[2,1024]{1,0:T(2,128)S(1)} %pad_maximum_fusion.4), channel_id=1, source_target_pairs={{0,8},{8,0},{16,24},{24,16},{32,40},{40,32},{48,56},{56,48},{1,9},... | collective-permute-start | bytes 24584 | tf_op jit(solution)/shard_map/ppermute | solution.py:1469
  391.2 7.4 %copy-start.17 = (bf16[256,1664]{1,0:T(8,128)(2,1)S(1)}, bf16[256,1664]{1,0:T(8,128)(2,1)}, u32[]{:S(2)}) copy-start(bf16[256,1664]{1,0:T(8,128)(2,1)} %get-tuple-element.45.refs_2_) | copy-start | bytes 2555908
  (16 other events, 25.9 us)
where the time goes:
time: 448 us; the launch traced here: 444 us
  Pallas kernels  334 us (75%)
  local copies, waits for them, and re-layouts  55.6 us (12%)
  matrix products  24.1 us (5%)
  other arithmetic  20.6 us (5%)
  starting transfers between devices  6.92 us (2%)
    pallas_call x2, Pallas kernels, attend_back(): pl.pallas_call(functools.partial(attend_back_kernel, with_reduce), name='...  139 us
    pallas_call x2, Pallas kernels, attend(): pl.pallas_call(functools.partial(attend_kernel, with_gather), name='atten...  104 us
    pallas_call x1, Pallas kernels, reduce_gradients(): pl.pallas_call(functools.partial(reduce_kernel, ATTENTION), name='reduce_...  40.5 us
    pallas_call x1, Pallas kernels, gather_weights(): pl.pallas_call(functools.partial(gather_kernel, ATTENTION), name='gather_...  28.7 us
    pallas_call x2, Pallas kernels, feed_back(): pl.pallas_call(feed_back_kernel, name='feed_back', grid=(blocks,), out_sh...  21.1 us
    unnamed x100, local copies, waits for them, and re-layouts  16.4 us
    dot_general x2, matrix products, forward_layer(): gated = jnp.dot(second_norm, gate_up, preferred_element_type=jnp.float32)  12.2 us
  transfers between devices with their start and end apart: 3, of which 0 were waited for; matrix products, arithmetic and copies ran while one was open for 8% of the time, Pallas kernels for 0%

commit v1 on v0

--- a/solution.py
+++ b/solution.py
@@ -1190,8 +1190,8 @@
 
 
 REDUCE_SPREAD = 2
-BACK_POINT = 3
-BACK_COLLECT = 8
+BACK_POINT = 5
+BACK_COLLECT = 13
 
 
 def attend_back(slope, kept, weight, tables, lefts=(), rights=()):
@@ -1277,6 +1277,31 @@
     )(down_in, down_weight, gate_up, gate_up, gated, gated)
 
 
+def begin_kernel(flags_ref, inputs_ref, cotangent_ref, fresh_ref, given_ref):
+    swapped = flags_ref[0]
+    fresh_ref[...] = jnp.zeros_like(fresh_ref)
+    given_ref[...] = jnp.zeros_like(given_ref)
+    for slot in range(SLOTS):
+        place = jnp.where(swapped == 1, 1 - slot, slot)
+        rows = slice(slot * LOCAL, (slot + 1) * LOCAL)
+        for shard in range(SHARDS):
+            have = slice(shard * ROWS, (shard + 1) * ROWS)
+            into = slice(shard * PADDED, shard * PADDED + ROWS)
+            fresh_ref[rows, into] = inputs_ref[place, :, have]
+            given_ref[rows, into] = cotangent_ref[slot, :, have]
+
+
+def begin(flags, inputs, cotangent):
+    return pl.pallas_call(
+        begin_kernel,
+        name="begin",
+        out_shape=[jax.ShapeDtypeStruct((ROWS_HERE, MODEL), jnp.bfloat16)] * 2,
+        in_specs=[pl.BlockSpec(memory_space=pltpu.SMEM)] + [VMEM] * 2,
+        out_specs=[VMEM] * 2,
+        compiler_params=pltpu.CompilerParams(vmem_limit_bytes=40 * 2**20),
+    )(flags, inputs, cotangent)
+
+
 def finish_kernel(
     flags_ref, hidden_slope_ref, values_ref, slope_ref, gain_ref, result_ref,
     grads_ref, outputs_ref, gain_slope_ref,
@@ -1383,7 +1408,7 @@
 def forward_layer(layer_in, tables, weights, shards=()):
     attend_in, attend_out, gate_up, down_weight, gains = weights
     rows = ROWS_HERE
-    values = layer_in.reshape(rows, MODEL).astype(jnp.float32)
+    values = layer_in.astype(jnp.float32)
     first_norm = normed(values, gains[0]).astype(jnp.bfloat16)
     mixed, *attended = attend(first_norm, attend_in, tables, shards)
     if shards:
@@ -1407,7 +1432,7 @@
         act,
     )
     weights = (attend_in, attend_out, gate_up, down_weight, gains)
-    return (result.astype(jnp.bfloat16).reshape(layer_in.shape), kept, weights)
+    return (result.astype(jnp.bfloat16), kept, weights)
 
 
 def backward_layer(upstream, kept, tables, weights, ending=None):
@@ -1423,10 +1448,8 @@
         gated,
         act,
     ) = kept
-    batches, local_count = upstream.shape[:2]
-    rows = batches * local_count
-    down_in = upstream.reshape(rows, MODEL)
-    upstream = down_in.astype(jnp.float32)
+    down_in = upstream
+    upstream = upstream.astype(jnp.float32)
     gated_slope, second_slope = feed_back(down_in, down_weight, gate_up, gated)
     hidden_part, second_gain = norm_backward(hidden, gains[1], second_slope)
     hidden_slope = upstream + hidden_part
@@ -1439,7 +1462,7 @@
         lefts = (second_norm, by_shard(act))
         rights = (gated_slope, down_in)
     projected_slope, first_slope, *summed = attend_back(
-        mixed_gradient.reshape(batches, local_count, FULL),
+        mixed_gradient.reshape(SLOTS, LOCAL, FULL),
         attended,
         attend_in,
         tables,
@@ -1448,10 +1471,10 @@
     )
     if not last:
         input_part, _ = norm_backward(values, gains[0], first_slope)
-        return (hidden_slope + input_part).reshape(batches, local_count, MODEL)
+        return hidden_slope + input_part
     flags, result = ending
     input_grads, outputs, first_gain = finish(
-        flags, hidden_slope, values, first_slope, gains[:1], result.reshape(rows, MODEL)
+        flags, hidden_slope, values, first_slope, gains[:1], result
     )
     gain_slopes = jnp.stack([first_gain[0], second_gain])
     lefts = (by_core(first_norm), by_core(padded(mixed[:, :QUERY_WIDTH])))
@@ -1517,16 +1540,15 @@
     def in_slots(values):
         return jnp.where(swap, values[::-1, 0], values[:, 0])
 
-    fresh = padded(in_slots(inputs))
+    flags = jnp.stack([swap, section_index == 0]).astype(jnp.int32)
+    fresh, given = begin(flags, inputs[:, 0], cotangent[:, 0])
     tables = rotary_tables(in_slots(positions))
-    given = padded(cotangent[:, 0])
     result, _, weights = forward_layer(fresh, tables, weights, shards)
     layer_in = jnp.where(section_index == 0, fresh, passed_along(result, 1))
     outputs, kept, _ = forward_layer(layer_in, tables, weights)
     input_slope = backward_layer(given, kept, tables, weights)
     back = passed_along(input_slope.astype(jnp.bfloat16), -1)
     upstream = jnp.where(section_index == 1, given, back)
-    flags = jnp.stack([swap, section_index == 0]).astype(jnp.int32)
     input_slopes, outputs, summed = backward_layer(
         upstream, kept, tables, weights, (flags, outputs)
     )

time: 448 us -> 453 us (1.011)
  waiting for transfers between devices: 0.01 us -> 12.7 us
  local copies, waits for them, and re-layouts: 55.6 us -> 48.3 us
    ppermute x2, waiting for transfers between devices: 0.01 us -> 12.7 us  [passed_along(): return lax.ppermute(value, 'section', [(0, 1)] if steps > 0 else [(1, 0)])]
    unnamed x100 -> x110, local copies, waits for them, and re-layouts: 16.4 us -> 23.7 us
    convert_element_type x3 -> x1, local copies, waits for them, and re-layouts: 7.26 us -> 2.05 us  [forward_layer(): first_norm = normed(values, gains[0]).astype(jnp.bfloat16)]
  transfers between devices with their start and end apart: 3 -> 3, of which waited for: 0 -> 2; matrix products, arithmetic and copies ran while one was open for 8% -> 5% of each run, Pallas kernels for 0% -> 0%
where the time goes in v1:
time: 453 us; the launch traced here: 449 us
  Pallas kernels  335 us (74%)
  local copies, waits for them, and re-layouts  48.3 us (11%)
  matrix products  27.3 us (6%)
  other arithmetic  16.9 us (4%)
  waiting for transfers between devices  12.7 us (3%)
  starting transfers between devices  7.18 us (2%)
    pallas_call x2, Pallas kernels, attend_back(): pl.pallas_call(functools.partial(attend_back_kernel, with_reduce), name='...  137 us
    pallas_call x2, Pallas kernels, attend(): pl.pallas_call(functools.partial(attend_kernel, with_gather), name='atten...  104 us
    pallas_call x1, Pallas kernels, reduce_gradients(): pl.pallas_call(functools.partial(reduce_kernel, ATTENTION), name='reduce_...  40.5 us
    pallas_call x1, Pallas kernels, gather_weights(): pl.pallas_call(functools.partial(gather_kernel, ATTENTION), name='gather_...  28.7 us
    unnamed x110, local copies, waits for them, and re-layouts  23.7 us
    pallas_call x2, Pallas kernels, feed_back(): pl.pallas_call(feed_back_kernel, name='feed_back', grid=(blocks,), out_sh...  20.7 us
    ppermute x2, waiting for transfers between devices, passed_along(): return lax.ppermute(value, 'section', [(0, 1)] if steps > 0 else [(1, 0)])  12.7 us
    dot_general x2, matrix products, forward_layer(): gated = jnp.dot(second_norm, gate_up, preferred_element_type=jnp.float32)  12 us
  transfers between devices with their start and end apart: 3, of which 2 were waited for; matrix products, arithmetic and copies ran while one was open for 5% of the time, Pallas kernels for 0%

profile of v1, /device:TPU:1, one launch (start us, length us, event | category | flops | bytes accessed | tf_op | source)
XLA Modules:
  0.0 449.0 jit_solution(17717774724910840772)
XLA Ops:
  2.7 2.0 copy.23
  4.7 2.0 copy.24
  9.2 28.7 %gather_weights.1 = (bf16[8,128,1664]{2,1,0:T(8,128)(2,1)}, bf16[8,128,1024]{2,1,0:T(8,128)(2,1)}) custom-call(bf16[128,1664]{1,0:T(8,128)(2,1)} %fusion.39.refs_0_, bf16[128,1024]{1,0:T(8,128)(2,1)} %pad.34.refs_1_), custom_call_target="tpu_custom_call" | custom-call | tf_op jit(solution)/shard_map/gather_weights/pallas_call | solution.py:286
  37.9 3.1 slice.80
  43.3 1.9 begin.1
  47.4 2.5 pad.35.refs_3_
  49.9 2.8 reshape_squeeze.7
  56.3 65.7 %attend_gather.1 = (bf16[2,128,1024]{2,1,0:T(8,128)(2,1)S(1)}, bf16[2,1024,128]{2,1,0:T(8,128)(2,1)}, bf16[2,2,1024,128]{3,2,1,0:T(8,128)(2,1)}, f32[2,1024,128]...) custom-call(bf16[256,1024]{1,0:T(8,128)(2,1)S(1)} %fusion.32.refs_0_, ...), custom_call_target="tpu_custom_call" | custom-call | tf_op jit(solution)/shard_map/attend_gather/pallas_call | solution.py:949
  122.1 2.2 multiply_reduce_fusion.6
  124.3 5.8 %fusion.35 = f32[256,5120]{1,0:T(8,128)S(1)} fusion(bf16[1024,5120]{1,0:T(8,128)(2,1)} %bitcast.109, f32[256,1024]{1,0:T(8,128)S(1)} %get-tuple-element.85, f32[1024]{0:T(1024)S(1)} %bitcast.136, f32[256]{0:T(256)S(1)} %add_rsqrt_fusion.2), kind=kOutput, calls=%fused_computation.46 | convolution fusion | flops 2685140992 | bytes 16782336 | tf_op jit(solution)/shard_map/dot_general | solution.py:1421
  130.1 2.5 fusion.27
  132.6 5.4 %collective-permute-start = (bf16[256,1024]{1,0:T(8,128)(2,1)}, bf16[256,1024]{1,0:T(8,128)(2,1)}, u32[]{:S(2)}, u32[]{:S(2)}) collective-permute-start(bf16[256,1024]{1,0:T(8,128)(2,1)} %fusion.27), channel_id=1, source_target_pairs={{0,64},{1,65},{2,66},{3,67},{4,68},{5,69},{6,70},{7,71},{8,72},{9,... | collective-permute-start | bytes 1572872 | tf_op jit(solution)/shard_map/ppermute | solution.py:1487
  138.0 10.8 %collective-permute-done = bf16[256,1024]{1,0:T(8,128)(2,1)} collective-permute-done((bf16[256,1024]{1,0:T(8,128)(2,1)}, bf16[256,1024]{1,0:T(8,128)(2,1)}, u32[]{:S(2)}, u32[]{:S(2)}) %collective-permute-start) | collective-permute-done | bytes 524320 | tf_op jit(solution)/shard_map/ppermute | solution.py:1487
  148.9 2.1 fusion.52
  152.8 38.3 %attend.1 = (bf16[2,128,1024]{2,1,0:T(8,128)(2,1)S(1)}, bf16[2,1024,128]{2,1,0:T(8,128)(2,1)S(1)}, bf16[2,2,1024,128]{3,2,1,0:T(8,128)(2,1)S(1)}, f32[2,1024,128]{2,1,0:T(8,128)S(1)}) custom-call(bf16[256,1024]{1,0:T(8,128)(2,1)S(1)} %multiply_convert_fusion.1.refs_0_, bf16[1024,1664]{1,0:T(8,128)(2,1)S(1)} %bitcast.87, f32[4,2,128,128]{3,2,1,0:T(8,128)S(1)} %copy-done.2), custom_call_target="tpu_custom_call" | custom-call | tf_op jit(solution)/shard_map/attend/pallas_call | solution.py:949
  194.7 2.1 copy.30
  196.7 2.6 multiply_reduce_fusion.4
  199.5 6.3 %fusion.53.gate_ref.up_ref = f32[256,5120]{1,0:T(8,128)S(1)} fusion(bf16[256,1024]{1,0:T(8,128)(2,1)S(1)} %multiply_convert_fusion.refs_6_, bf16[1024,5120]{1,0:T(8,128)(2,1)} %bitcast.110), kind=kOutput, calls=%fused_computation.91 | convolution fusion | flops 2684354560 | bytes 16252928 | tf_op jit(solution)/shard_map/dot_general | solution.py:1421
  205.8 2.3 fusion
  208.5 10.8 %feed_back.2 = (bf16[2,256,2560]{2,1,0:T(8,128)(2,1)}, f32[256,1024]{1,0:T(8,128)S(1)}) custom-call(bf16[256,1024]{1,0:T(8,128)(2,1)S(1)} %copy-done.6, bf16[2560,1024]{1,0:T(8,128)(2,1)S(1)} %bitcast.94, bf16[1024,5120]{1,0:T(8,128)(2,1)} %bitcast.111, bf16[1024,5120]{1,0:T(8,128)(2,1)} %bitcast.112, f32[256,5120]{1,0:T(8,128)} %copy-done.27, ...), custom_call_target="tpu_custom_call" | custom-call | tf_op jit(solution)/shard_map/feed_back/pallas_call | solution.py:1259
  221.5 32.7 %attend_back.1 = (bf16[256,1664]{1,0:T(8,128)(2,1)}, f32[256,1024]{1,0:T(8,128)S(1)}) custom-call(bf16[2,128,1024]{2,1,0:T(8,128)(2,1)S(1)} %bitcast.103, bf16[2,1024,128]{2,1,0:T(8,128)(2,1)S(1)} %copy-done.17, bf16[2,2,1024,128]{3,2,1,0:T(8,128)(2,1)S(1)} %copy-done.10, f32[2,1024,128]{2,1,0:T(8,128)S(1)} %copy-done.12, bf16[1024,1664]{1,0:T(8,128)(2,1)} %bitcast.84, ...), custom_call_target="tpu_custom_call" | custom-call | tf_op jit(solution)/shard_map/attend_back/pallas_call | solution.py:1200
  258.0 1.6 copy.29
  261.7 5.6 %fusion.20.result_ref = bf16[256,1024]{1,0:T(8,128)(2,1)} fusion(f32[256,1024]{1,0:T(8,128)} %copy-done.28, bf16[256,2560]{1,0:T(8,128)(2,1)} %fusion, bf16[2560,1024]{1,0:T(8,128)(2,1)} %bitcast.88), kind=kOutput, calls=%fused_computation.19 | convolution fusion | flops 1342701568 | bytes 8126464 | tf_op jit(solution)/shard_map/dot_general | solution.py:1423
  267.4 1.9 collective-permute-done.1
  270.4 9.8 %feed_back.3 = (bf16[2,256,2560]{2,1,0:T(8,128)(2,1)S(1)}, f32[256,1024]{1,0:T(8,128)S(1)}) custom-call(bf16[256,1024]{1,0:T(8,128)(2,1)S(1)} %broadcast_select_fusion.1.slope_ref.refs_9_, bf16[2560,1024]{1,0:T(8,128)(2,1)S(1)} %bitcast.97, bf16[1024,5120]{1,0:T(8,128)(2,1)} %bitcast.113, bf16[1024,5120]{1,0:T(8,128)(2,1)} %bitcast.114, ...), custom_call_target="tpu_custom_call" | custom-call | tf_op jit(solution)/shard_map/feed_back/pallas_call | solution.py:1259
  282.7 1.5 fusion.24
  284.3 104.6 %attend_back_reduce.1 = (bf16[256,1664]{1,0:T(8,128)(2,1)}, f32[256,1024]{1,0:T(8,128)}, bf16[128,5120]{1,0:T(8,128)(2,1)}, bf16[320,1024]{1,0:T(8,128)(2,1)}) custom-call(bf16[2,128,1024]{2,1,0:T(8,128)(2,1)} %bitcast.135, bf16[2,1024,128]{2,1,0:T(8,128)(2,1)} %copy-done.16, bf16[2,2,1024,128]{3,2,1,0:T(8,128)(2,1)} %copy-done.9, ...), custom_call_target="tpu_custom_call" | custom-call | tf_op jit(solution)/shard_map/attend_back_reduce/pallas_call | solution.py:1200
  393.1 1.7 bitcast_convert_fusion
  396.1 2.1 copy.37
  398.2 2.5 copy.38
  400.7 2.9 reshape.174
  404.8 40.5 %reduce_gradients.1 = (bf16[128,1664]{1,0:T(8,128)(2,1)S(1)}, bf16[128,1024]{1,0:T(8,128)(2,1)S(1)}) custom-call(bf16[2,8,256,64]{3,2,1,0:T(8,128)(2,1)S(1)} %bitcast.98, bf16[2,8,256,64]{3,2,1,0:T(8,128)(2,1)S(1)} %bitcast.99, bf16[256,1664]{1,0:T(8,128)(2,1)S(1)} %copy-done.22, bf16[256,1024]{1,0:T(8,128)(2,1)S(1)} %get-tuple-element.71.refs_3_, ...), custom_call_target="tpu_custom_call" | custom-call | tf_op jit(solution)/shard_map/reduce_gradients/pallas_call | solution.py:681
  (174 shorter events, 39.5 us)
Async XLA Ops:
  0.6 6.5 %copy-start.40 = (bf16[1,120,960]{2,1,0:T(8,128)(2,1)S(1)}, bf16[1,120,960]{2,1,0:T(8,128)(2,1)}, u32[]{:S(2)}) copy-start(bf16[1,120,960]{2,1,0:T(8,128)(2,1)} %param.13) | copy-start | bytes 691204
  4.7 3.7 copy-start.42
  8.4 32.7 %copy-start.43 = (s32[1,2]{1,0:T(1,128)S(1)}, s32[1,2]{1,0:T(1,128)}, u32[]{:S(2)}) copy-start(s32[1,2]{1,0:T(1,128)} %param.11) | copy-start | bytes 28
  37.9 3.1 copy-start
  49.9 5.5 %copy-start.41 = (s32[2,1,128]{2,1,0:T(1,128)S(1)}, s32[2,1,128]{2,1,0:T(1,128)}, u32[]{:S(2)}) copy-start(s32[2,1,128]{2,1,0:T(1,128)} %param.10) | copy-start | bytes 3076
  52.7 3.6 copy-start.7
  56.3 65.8 %copy-start.1 = (f32[4,2,128,128]{3,2,1,0:T(8,128)}, f32[4,2,128,128]{3,2,1,0:T(8,128)S(1)}, u32[]{:S(2)}) copy-start(f32[4,2,128,128]{3,2,1,0:T(8,128)S(1)} %pad_maximum_fusion.1.refs_2_.refs_5_) | copy-start | bytes 1572868
  56.3 65.8 %copy-start.32 = (bf16[8,120,1024]{2,1,0:T(8,128)(2,1)S(1)}, bf16[8,120,1024]{2,1,0:T(8,128)(2,1)}, u32[]{:S(2)}) copy-start(bf16[8,120,1024]{2,1,0:T(8,128)(2,1)} %slice.80) | copy-start | bytes 5898244
  122.1 8.0 %slice-start = ((s8[5242880]{0:T(1024)(128)(4,1)}), s8[4194304]{0:T(1024)(128)(4,1)S(1)}, s32[]{:S(2)}) async-start(s8[5242880]{0:T(1024)(128)(4,1)} %bitcast.89), calls=%async_computation | async-start | bytes 8388608
  124.3 5.8 %slice-start.1 = ((s8[5242880]{0:T(1024)(128)(4,1)}), s8[1048576]{0:T(1024)(128)(4,1)S(1)}, s32[]{:S(2)}) async-start(s8[5242880]{0:T(1024)(128)(4,1)} %bitcast.89), calls=%async_computation.1 | async-start | bytes 2097152
  132.6 16.2 %collective-permute-start = (bf16[256,1024]{1,0:T(8,128)(2,1)}, bf16[256,1024]{1,0:T(8,128)(2,1)}, u32[]{:S(2)}, u32[]{:S(2)}) collective-permute-start(bf16[256,1024]{1,0:T(8,128)(2,1)} %fusion.27), channel_id=1, source_target_pairs={{0,64},{1,65},{2,66},{3,67},{4,68},{5,69},{6,70},{7,71},{8,72},{9,... | collective-permute-start | bytes 1572872 | tf_op jit(solution)/shard_map/ppermute | solution.py:1487
  138.0 14.7 %copy-start.2 = (f32[4,2,128,128]{3,2,1,0:T(8,128)S(1)}, f32[4,2,128,128]{3,2,1,0:T(8,128)}, u32[]{:S(2)}) copy-start(f32[4,2,128,128]{3,2,1,0:T(8,128)} %copy-done.1) | copy-start | bytes 1572868
  199.3 55.2 %copy-start.28 = (f32[256,1024]{1,0:T(8,128)}, f32[256,1024]{1,0:T(8,128)S(1)}, u32[]{:S(2)}) copy-start(f32[256,1024]{1,0:T(8,128)S(1)} %get-tuple-element.87) | copy-start | bytes 3145732
  199.4 9.2 %slice-start.2 = ((s8[5242880]{0:T(1024)(128)(4,1)}), s8[4194304]{0:T(1024)(128)(4,1)S(1)}, s32[]{:S(2)}) async-start(s8[5242880]{0:T(1024)(128)(4,1)} %bitcast.92), calls=%async_computation.2 | async-start | bytes 8388608
  199.5 6.3 %copy-start.36 = (bf16[256,1024]{1,0:T(8,128)(2,1)}, bf16[256,1024]{1,0:T(8,128)(2,1)S(1)}, u32[]{:S(2)}) copy-start(bf16[256,1024]{1,0:T(8,128)(2,1)S(1)} %multiply_convert_fusion.refs_6_) | copy-start | bytes 1572868
  199.5 9.0 %slice-start.3 = ((s8[5242880]{0:T(1024)(128)(4,1)}), s8[1048576]{0:T(1024)(128)(4,1)S(1)}, s32[]{:S(2)}) async-start(s8[5242880]{0:T(1024)(128)(4,1)} %bitcast.92), calls=%async_computation.3 | async-start | bytes 2097152
  205.8 2.7 copy-start.27
  205.8 2.7 copy-start.6
  208.5 11.2 %copy-start.33 = (bf16[8,120,1024]{2,1,0:T(8,128)(2,1)S(1)}, bf16[8,120,1024]{2,1,0:T(8,128)(2,1)}, u32[]{:S(2)}) copy-start(bf16[8,120,1024]{2,1,0:T(8,128)(2,1)} %slice.80) | copy-start | bytes 5898244
  221.5 32.7 %copy-start.31 = (bf16[256,1024]{1,0:T(8,128)(2,1)S(1)}, bf16[256,1024]{1,0:T(8,128)(2,1)}, u32[]{:S(2)}) copy-start(bf16[256,1024]{1,0:T(8,128)(2,1)} %copy-done.30) | copy-start | bytes 1572868
  254.5 2.7 copy-start.35
  255.9 13.3 %collective-permute-start.1 = (bf16[256,1024]{1,0:T(8,128)(2,1)}, bf16[256,1024]{1,0:T(8,128)(2,1)}, u32[]{:S(2)}, u32[]{:S(2)}) collective-permute-start(bf16[256,1024]{1,0:T(8,128)(2,1)} %add_convert_fusion), channel_id=1, source_target_pairs={{64,0},{65,1},{66,2},{67,3},{68,4},{69,5},{70,6},{71,7},{72,8},{73... | collective-permute-start | bytes 1572872 | tf_op jit(solution)/shard_map/ppermute | solution.py:1487
  260.4 10.0 %slice-start.4 = ((s8[5242880]{0:T(1024)(128)(4,1)}), s8[1048576]{0:T(1024)(128)(4,1)S(1)}, s32[]{:S(2)}) async-start(s8[5242880]{0:T(1024)(128)(4,1)} %bitcast.95), calls=%async_computation.4 | async-start | bytes 2097152
  261.7 8.6 %slice-start.5 = ((s8[5242880]{0:T(1024)(128)(4,1)}), s8[4194304]{0:T(1024)(128)(4,1)S(1)}, s32[]{:S(2)}) async-start(s8[5242880]{0:T(1024)(128)(4,1)} %bitcast.95), calls=%async_computation.5 | async-start | bytes 8388608
  270.4 10.3 %copy-start.4 = (bf16[256,1024]{1,0:T(8,128)(2,1)}, bf16[256,1024]{1,0:T(8,128)(2,1)S(1)}, u32[]{:S(2)}) copy-start(bf16[256,1024]{1,0:T(8,128)(2,1)S(1)} %broadcast_select_fusion.1.slope_ref.refs_9_) | copy-start | bytes 1572868
  270.4 9.9 %copy-start.29 = (f32[256,1024]{1,0:T(8,128)S(1)}, f32[256,1024]{1,0:T(8,128)}, u32[]{:S(2)}) copy-start(f32[256,1024]{1,0:T(8,128)} %copy-done.28) | copy-start | bytes 3145732
  284.3 104.6 %copy-start.13 = (f32[256,1024]{1,0:T(8,128)S(1)}, f32[256,1024]{1,0:T(8,128)}, u32[]{:S(2)}) copy-start(f32[256,1024]{1,0:T(8,128)} %get-tuple-element.73.values_ref) | copy-start | bytes 3145732
  392.6 3.5 copy-start.26
  392.6 3.5 copy-start.21
  392.6 2.2 copy-start.39
  392.6 11.0 %collective-permute-start.2 = (f32[2,1024]{1,0:T(2,128)S(1)}, f32[2,1024]{1,0:T(2,128)S(1)}, u32[]{:S(2)}, u32[]{:S(2)}) collective-permute-start(f32[2,1024]{1,0:T(2,128)S(1)} %pad_maximum_fusion.4), channel_id=1, source_target_pairs={{0,8},{8,0},{16,24},{24,16},{32,40},{40,32},{48,56},{56,48},{1,9},... | collective-permute-start | bytes 24584 | tf_op jit(solution)/shard_map/ppermute | solution.py:1492
  396.1 7.5 %copy-start.14 = (bf16[256,8,2,64]{3,0,1,2:T(8,128)(2,1)S(1)}, bf16[256,8,2,64]{3,0,1,2:T(8,128)(2,1)}, u32[]{:S(2)}) copy-start(bf16[256,8,2,64]{3,0,1,2:T(8,128)(2,1)} %copy.33) | copy-start | bytes 1572868
  (21 other events, 26.7 us)
